TPU v7x, 32 devices: a whole 2x2x4 slice. The times are simulated.
32 devices in a mesh: seq: 8 (over z, y), fsdp: 4 (over x, core).
Axes of the slice: x: 2, y: 2, z: 4, core: 2. Of those that a mesh axis runs over, the one named last changes fastest.
Arguments:
- tokens: bfloat16 [4, 8192, 768], P('fsdp', 'seq'), may hold values from -6 to 6
- in_weight: bfloat16 [768, 3352], P('fsdp'), may hold values from -0.21875 to 0.21875
- out_weight: bfloat16 [1536, 768], P('fsdp'), may hold values from -0.15625 to 0.15625
- conv_weight: bfloat16 [1792, 4], P('fsdp'), may hold values from -3 to 3
- conv_bias: bfloat16 [1792], P('fsdp'), may hold values from -3 to 3
- step_bias: bfloat16 [24], P('fsdp'), may hold values from -4 to -1
- decay_param: bfloat16 [24], P('fsdp'), may hold values from -7 to -0.5
- skip_gain: bfloat16 [24], P('fsdp'), may hold values from 0.5 to 1.5
- norm_gain: bfloat16 [768], P('fsdp'), may hold values from 0.099609375 to 1.8984375
- gate_gain: bfloat16 [1536], P('fsdp'), may hold values from 0.099609375 to 1.8984375
- cotangent: bfloat16 [4, 8192, 768], P('fsdp', 'seq'), may hold values from -6 to 6
Outputs:
- block_out: bfloat16 [4, 8192, 768], P('fsdp', 'seq')
- grad_input: bfloat16 [4, 8192, 768], P('fsdp', 'seq')
- grad_inproj: float32 [768, 3352], P('fsdp')
- grad_outproj: float32 [1536, 768], P('fsdp')
- grad_conv: float32 [1792, 4], P('fsdp')
- grad_convbias: float32 [1792], P('fsdp')
- grad_stepbias: float32 [24], P('fsdp')
- grad_decay: float32 [24], P('fsdp')
- grad_skip: float32 [24], P('fsdp')
- grad_normgain: float32 [768], P('fsdp')
- grad_gategain: float32 [1536], P('fsdp')
All inputs are finite; a program needn't handle non-finite values.
Results may differ from a plain program's by a relative error of at most 0.0033.
The roundings to bfloat16 on the way count: a program that leaves them out, or rounds other values in their place, can miss the bound.
Values may be sent and summed in bfloat16 or wider, within the bound.
A program may use at most 256 MiB of HBM per device.

v0:
```python
import jax
import jax.numpy as jnp
from jax import lax
from jax.sharding import PartitionSpec as P

SPAN = 256


epsilon = 1e-05
highest = lax.Precision.HIGHEST


def from_behind(array, axis, by):
    devices = lax.axis_size(axis)
    pairs = [(i, i + by) for i in range(devices) if 0 <= i + by < devices]
    return lax.ppermute(array, axis, pairs)


def prefix(part, axis, combine, identity, reverse):
    count = lax.axis_size(axis)
    place = lax.axis_index(axis)
    ahead = count - 1 - place if reverse else place
    gathered = jax.tree.map(lambda a: lax.all_gather(a, axis), part)
    state = jax.tree.map(lambda a, e: jnp.zeros_like(a) + jnp.asarray(e, a.dtype), part, identity)

    def one(lap, state):
        source = count - 1 - lap if reverse else lap
        return combine(
            state, jax.tree.map(lambda a: lax.dynamic_index_in_dim(a, source, 0, False), gathered)
        )

    return lax.fori_loop(0, ahead, one, state)


def silu_slope(inputs):
    sig_value = jax.nn.sigmoid(inputs)
    return sig_value * (1.0 + inputs * (1.0 - sig_value))


def link_states(earlier, following):
    return (
        earlier[0] + following[0],
        jnp.exp(following[0])[:, None, None] * earlier[1] + following[1],
    )


def span_kernel(cumulative):
    positions = jnp.arange(cumulative.shape[0])
    causal = (positions[:, None] >= positions[None, :])[:, :, None]
    spread = jnp.where(causal, cumulative[:, None, :] - cumulative[None, :, :], 0.0)
    return jnp.where(causal, jnp.exp(spread), 0.0)


def span_forward(pieces):
    values, write_rows, read_rows, dt_step, cumulative, entering = pieces
    kernel = span_kernel(cumulative)
    scores = jnp.dot(read_rows, write_rows.T, precision=highest)
    weights = scores[:, :, None] * kernel * dt_step[None, :, :]
    inner_part = jnp.einsum("tsh,shp->thp", weights, values, precision=highest)
    carried = jnp.exp(cumulative)[:, :, None] * jnp.einsum(
        "tn,hpn->thp", read_rows, entering, precision=highest
    )
    return inner_part + carried


def span_backward(pieces):
    (
        values,
        write_rows,
        read_rows,
        dt_step,
        cumulative,
        entering,
        grad_mixed,
        grad_state,
        grad_total,
    ) = pieces
    kernel = span_kernel(cumulative)
    scores = jnp.dot(read_rows, write_rows.T, precision=highest)
    weights = scores[:, :, None] * kernel * dt_step[None, :, :]
    grad_weights = jnp.einsum("thp,shp->tsh", grad_mixed, values, precision=highest)
    grad_values = jnp.einsum("tsh,thp->shp", weights, grad_mixed, precision=highest)
    products = grad_weights * weights
    grad_scores = jnp.sum(grad_weights * kernel * dt_step[None, :, :], axis=2)
    grad_read = jnp.dot(grad_scores, write_rows, precision=highest)
    grad_write = jnp.einsum("ts,tn->sn", grad_scores, read_rows, precision=highest)
    grad_step = jnp.sum(grad_weights * scores[:, :, None] * kernel, axis=0)
    grad_cumul = jnp.sum(products, axis=1) - jnp.sum(products, axis=0)
    growth = jnp.exp(cumulative)
    carried_raw = jnp.einsum("tn,hpn->thp", read_rows, entering, precision=highest)
    grad_read = grad_read + jnp.einsum(
        "th,thp,hpn->tn", growth, grad_mixed, entering, precision=highest
    )
    grad_cumul = grad_cumul + growth * jnp.sum(grad_mixed * carried_raw, axis=2)
    fading = jnp.exp(cumulative[-1][None, :] - cumulative)
    tail_weight = fading * dt_step
    state_rows = jnp.einsum("hpn,sn->shp", grad_state, write_rows, precision=highest)
    grad_values = grad_values + tail_weight[:, :, None] * state_rows
    grad_write = grad_write + jnp.einsum(
        "sh,shp,hpn->sn", tail_weight, values, grad_state, precision=highest
    )
    grad_tail = jnp.sum(state_rows * values, axis=2)
    grad_step = grad_step + grad_tail * fading
    flowing = grad_tail * tail_weight
    grad_cumul = grad_cumul - flowing
    grad_cumul = grad_cumul.at[-1].add(jnp.sum(flowing, axis=0) + grad_total)
    grad_decay = jnp.cumsum(grad_cumul[::-1], axis=0)[::-1]
    return (grad_values, grad_write, grad_read, grad_step, grad_decay)


def advance(state, pieces):
    total_log, contrib = pieces
    return (jnp.exp(total_log)[:, None, None] * state + contrib, state)


def retreat(grad_next, pieces):
    total_log, direct_here = pieces
    grad_here = direct_here + jnp.exp(total_log)[:, None, None] * grad_next
    return (grad_here, grad_next)


def on_device(
    tokens,
    in_weight,
    out_weight,
    conv_weight,
    conv_bias,
    step_bias,
    decay_param,
    skip_gain,
    norm_gain,
    gate_gain,
    cotangent,
):
    (
        full_in,
        full_out,
        full_conv,
        full_bias,
        full_step,
        full_decay,
        full_skip,
        full_norm,
        full_gate,
    ) = (
        lax.all_gather(in_weight, "fsdp", axis=0, tiled=True),
        lax.all_gather(out_weight, "fsdp", axis=0, tiled=True),
        lax.all_gather(conv_weight, "fsdp", axis=0, tiled=True),
        lax.all_gather(conv_bias, "fsdp", axis=0, tiled=True),
        lax.all_gather(step_bias, "fsdp", axis=0, tiled=True),
        lax.all_gather(decay_param, "fsdp", axis=0, tiled=True),
        lax.all_gather(skip_gain, "fsdp", axis=0, tiled=True),
        lax.all_gather(norm_gain, "fsdp", axis=0, tiled=True),
        lax.all_gather(gate_gain, "fsdp", axis=0, tiled=True),
    )
    length = tokens.shape[1]
    head_count = full_step.shape[0]
    inner_width = full_out.shape[0]
    conv_width = full_conv.shape[0]
    tap_count = full_conv.shape[1]
    state_dim = (conv_width - inner_width) // 2
    head_dim = inner_width // head_count
    span_count = length // SPAN
    conv_taps = full_conv.astype(jnp.float32)
    conv_offset = full_bias.astype(jnp.float32)
    step_offset = full_step.astype(jnp.float32)
    decay_values = full_decay.astype(jnp.float32)
    skip_values = full_skip.astype(jnp.float32)
    gain_in = full_norm.astype(jnp.float32)
    gain_out = full_gate.astype(jnp.float32)
    source = tokens[0].astype(jnp.float32)
    in_scale = lax.rsqrt(jnp.mean(source * source, axis=1, keepdims=True) + epsilon)
    normed = (source * in_scale * gain_in).astype(jnp.bfloat16)
    projected = jnp.dot(normed, full_in, preferred_element_type=jnp.float32).astype(jnp.bfloat16)
    gate_part = projected[:, :inner_width].astype(jnp.float32)
    conv_in = projected[:, inner_width : inner_width + conv_width]
    step_raw = projected[:, inner_width + conv_width :].astype(jnp.float32)
    rim_rows = from_behind(conv_in[length - (tap_count - 1) :], "seq", 1)
    extended = jnp.concatenate([rim_rows, conv_in], axis=0).astype(jnp.float32)
    conv_sum = conv_offset[None, :] + jnp.zeros((length, conv_width), jnp.float32)
    for tap_index in range(tap_count):
        conv_sum = conv_sum + conv_taps[:, tap_index] * extended[tap_index : tap_index + length]
    conv_out = jax.nn.silu(conv_sum)
    values = conv_out[:, :inner_width].reshape(length, head_count, head_dim)
    write_rows = conv_out[:, inner_width : inner_width + state_dim]
    read_rows = conv_out[:, inner_width + state_dim :]
    step_pre = step_raw + step_offset
    dt_step = jax.nn.softplus(step_pre)
    decay_rate = -jnp.exp(decay_values)
    decay_log = dt_step * decay_rate
    span_values = values.reshape(span_count, SPAN, head_count, head_dim)
    span_write = write_rows.reshape(span_count, SPAN, state_dim)
    span_read = read_rows.reshape(span_count, SPAN, state_dim)
    span_step = dt_step.reshape(span_count, SPAN, head_count)
    cumulative = jnp.cumsum(decay_log.reshape(span_count, SPAN, head_count), axis=1)
    span_log = cumulative[:, -1]
    tail_weight = jnp.exp(span_log[:, None, :] - cumulative) * span_step
    span_state = jnp.einsum(
        "cqh,cqhp,cqn->chpn", tail_weight, span_values, span_write, precision=highest
    )
    empty_state = jnp.zeros((head_count, head_dim, state_dim), jnp.float32)
    empty_log = jnp.zeros((head_count,), jnp.float32)
    final_local, entering_zero = lax.scan(advance, empty_state, (span_log, span_state))
    device_log = jnp.sum(span_log, axis=0)
    _, incoming = prefix(
        (device_log, final_local), "seq", link_states, (empty_log, empty_state), False
    )
    prior_log = jnp.cumsum(span_log, axis=0) - span_log
    entering = entering_zero + jnp.exp(prior_log)[:, :, None, None] * incoming
    mixed = lax.map(
        span_forward, (span_values, span_write, span_read, span_step, cumulative, entering)
    )
    mixed = mixed.reshape(length, head_count, head_dim) + skip_values[None, :, None] * values
    flat = mixed.reshape(length, inner_width)
    gate_silu = jax.nn.silu(gate_part)
    gated = flat * gate_silu
    gate_scale = lax.rsqrt(jnp.mean(gated * gated, axis=1, keepdims=True) + epsilon)
    normed_out = (gated * gate_scale * gain_out).astype(jnp.bfloat16)
    block_out = source + jnp.dot(normed_out, full_out, preferred_element_type=jnp.float32)
    grad_out = cotangent[0]
    grad_outproj = jnp.einsum("ti,td->id", normed_out, grad_out, preferred_element_type=jnp.float32)
    grad_normed = jnp.einsum("td,id->ti", grad_out, full_out, preferred_element_type=jnp.float32)
    grad_gategain = jnp.sum(grad_normed * gated * gate_scale, axis=0)
    grad_scaled = grad_normed * gain_out
    grad_gated = gate_scale * grad_scaled - gated * gate_scale**3 * jnp.mean(
        grad_scaled * gated, axis=1, keepdims=True
    )
    grad_gate = grad_gated * flat * silu_slope(gate_part)
    grad_mixed = (grad_gated * gate_silu).reshape(length, head_count, head_dim)
    grad_skip = jnp.sum(grad_mixed * values, axis=(0, 2))
    span_grad = grad_mixed.reshape(span_count, SPAN, head_count, head_dim)
    direct = jnp.einsum(
        "cqh,cqhp,cqn->chpn", jnp.exp(cumulative), span_grad, span_read, precision=highest
    )
    start_grad, after_zero = lax.scan(retreat, empty_state, (span_log, direct), reverse=True)
    _, outgoing = prefix(
        (device_log, start_grad), "seq", link_states, (empty_log, empty_state), True
    )
    after_log = device_log[None, :] - jnp.cumsum(span_log, axis=0)
    leaving = after_zero + jnp.exp(after_log)[:, :, None, None] * outgoing
    grad_total = jnp.sum(leaving * jnp.exp(span_log)[:, :, None, None] * entering, axis=(2, 3))
    grad_values, grad_write, grad_read, grad_step, grad_decaylog = lax.map(
        span_backward,
        (
            span_values,
            span_write,
            span_read,
            span_step,
            cumulative,
            entering,
            span_grad,
            leaving,
            grad_total,
        ),
    )
    grad_values = (
        grad_values.reshape(length, head_count, head_dim) + skip_values[None, :, None] * grad_mixed
    )
    grad_decaylog = grad_decaylog.reshape(length, head_count)
    grad_step = grad_step.reshape(length, head_count) + grad_decaylog * decay_rate
    grad_decay = jnp.sum(grad_decaylog * dt_step, axis=0) * decay_rate
    grad_pre = grad_step * jax.nn.sigmoid(step_pre)
    grad_stepbias = jnp.sum(grad_pre, axis=0)
    grad_convout = jnp.concatenate(
        [
            grad_values.reshape(length, inner_width),
            grad_write.reshape(length, state_dim),
            grad_read.reshape(length, state_dim),
        ],
        axis=1,
    )
    grad_sum = grad_convout * silu_slope(conv_sum)
    grad_convbias = jnp.sum(grad_sum, axis=0)
    grad_conv = jnp.stack(
        [
            jnp.sum(grad_sum * extended[tap_index : tap_index + length], axis=0)
            for tap_index in range(tap_count)
        ],
        axis=1,
    )
    grad_extended = jnp.zeros((length + tap_count - 1, conv_width), jnp.float32)
    for tap_index in range(tap_count):
        grad_extended = grad_extended.at[tap_index : tap_index + length].add(
            conv_taps[:, tap_index] * grad_sum
        )
    rim_grad = from_behind(grad_extended[: tap_count - 1], "seq", -1)
    grad_conv_in = grad_extended[tap_count - 1 :] + jnp.pad(
        rim_grad, ((length - (tap_count - 1), 0), (0, 0))
    )
    grad_projected = jnp.concatenate([grad_gate, grad_conv_in, grad_pre], axis=1).astype(
        jnp.bfloat16
    )
    grad_inproj = jnp.einsum(
        "td,tk->dk", normed, grad_projected, preferred_element_type=jnp.float32
    )
    grad_normed_in = jnp.einsum(
        "tk,dk->td", grad_projected, full_in, preferred_element_type=jnp.float32
    )
    grad_normgain = jnp.sum(grad_normed_in * source * in_scale, axis=0)
    grad_scaled_in = grad_normed_in * gain_in
    grad_source = in_scale * grad_scaled_in - source * in_scale**3 * jnp.mean(
        grad_scaled_in * source, axis=1, keepdims=True
    )
    grad_source = grad_source + grad_out.astype(jnp.float32)
    parted = (
        lax.psum_scatter(grad_inproj, "fsdp", scatter_dimension=0, tiled=True),
        lax.psum_scatter(grad_outproj, "fsdp", scatter_dimension=0, tiled=True),
        lax.psum_scatter(grad_conv, "fsdp", scatter_dimension=0, tiled=True),
        lax.psum_scatter(grad_convbias, "fsdp", scatter_dimension=0, tiled=True),
        lax.psum_scatter(grad_stepbias, "fsdp", scatter_dimension=0, tiled=True),
        lax.psum_scatter(grad_decay, "fsdp", scatter_dimension=0, tiled=True),
        lax.psum_scatter(grad_skip, "fsdp", scatter_dimension=0, tiled=True),
        lax.psum_scatter(grad_normgain, "fsdp", scatter_dimension=0, tiled=True),
        lax.psum_scatter(grad_gategain, "fsdp", scatter_dimension=0, tiled=True),
    )
    shares = lax.psum(
        (
            parted[0],
            parted[1],
            parted[2],
            parted[3],
            parted[4],
            parted[5],
            parted[6],
            parted[7],
            parted[8],
        ),
        "seq",
    )
    return (
        block_out[None].astype(jnp.bfloat16),
        grad_source[None].astype(jnp.bfloat16),
        shares[0],
        shares[1],
        shares[2],
        shares[3],
        shares[4],
        shares[5],
        shares[6],
        shares[7],
        shares[8],
    )


def solution(mesh):
    placed = (
        P("fsdp", "seq", None),
        P("fsdp", None),
        P("fsdp", None),
        P("fsdp", None),
        P("fsdp"),
        P("fsdp"),
        P("fsdp"),
        P("fsdp"),
        P("fsdp"),
        P("fsdp"),
        P("fsdp", "seq", None),
    )
    return jax.shard_map(
        on_device,
        mesh=mesh,
        in_specs=placed,
        out_specs=(
            P("fsdp", "seq", None),
            P("fsdp", "seq", None),
            P("fsdp", None),
            P("fsdp", None),
            P("fsdp", None),
            P("fsdp"),
            P("fsdp"),
            P("fsdp"),
            P("fsdp"),
            P("fsdp"),
            P("fsdp"),
        ),
        check_vma=False,
    )
```

profile of v0, /device:TPU:0, one launch (start us, length us, event | category | flops | bytes accessed | tf_op | source)
XLA Modules:
  0.0 1366.0 jit_solution(15512095323494734569)
XLA Ops:
  15.5 8.5 all-reduce.17
  24.1 5.4 all-gather.3
  32.1 21.2 %all-gather.10.cloned.1.call-done = bf16[768,3352]{1,0:T(8,128)(2,1)} async-done(((bf16[192,3352]{1,0:T(8,128)(2,1)}), bf16[768,3352]{1,0:T(8,128)(2,1)}) %all-gather.10.cloned.1.call-update) | async-done | bytes 5148688 | tf_op jit(solution)/shard_map/all_gather | solution.py:146
  53.3 9.0 convolution_convert_fusion
  72.1 9.8 collective-permute-done
  84.4 9.0 fusion.105
  98.5 8.1 reshape_reshape.6
  106.6 10.2 fusion.115
  118.8 9.0 while.95
  130.3 5.1 all-gather.4
  136.4 23.0 %all-reduce.6 = f32[192]{0:T(256)S(1)} all-reduce(f32[192]{0:T(256)S(1)} %dynamic-update-slice.22), channel_id=2, replica_groups=mesh['seq'=8,'fsdp'=4] {'seq'}, use_global_device_ids=true, to_apply=%add.6 | all-reduce | flops 192 | bytes 1536
  161.2 6.6 copy.240
  169.1 60.2 %all-gather.14.cloned.1.call-done = f32[192,64,128]{2,1,0:T(8,128)} async-done(((f32[24,64,128]{2,1,0:T(8,128)}), f32[192,64,128]{2,1,0:T(8,128)}) %all-gather.14.cloned.1.call-update) | async-done | bytes 6291472 | tf_op jit(solution)/shard_map/all_gather | solution.py:23
  237.8 196.0 %while.92 = (s32[]{:T(128)}, f32[4,256,24,64]{1,0,3,2:T(4,128)}, f32[4,256,24,64]{1,3,2,0:T(8,128)}, f32[4,256,128]{2,1,0:T(8,128)}, f32[4,256,128]{2,1,0:T(8,12...) while((s32[]{:T(128)}, f32[4,256,24,64]{1,0,3,2:T(4,128)}, ...), condition=%wide.region_10.11_spmd, body=%wide.region_9.10_spmd.sunk | while | flops 1921318912 | bytes 14641777 | solution.py:210
  239.3 8.8 fusion.207
  252.3 34.5 %dynamic_update_slice.63 = f32[4,256,24,64]{1,0,3,2:T(4,128)} dynamic-update-slice(f32[4,256,24,64]{1,0,3,2:T(4,128)} %get-tuple-element.1290, f32[1,256,24,64]{1,0,3,2:T(1,128)S(1)} %copy.348, s32[]{:T(128)} %get-tuple-element.1289, s32[]{:T(128)} %constant.337.clone.1..sunk.1, s32[]{:T(128)} %constant.337.clone.1..sunk.1, s32[]{:T(128)} %constant.337.clone.1..sunk.1) | dynamic-update-slice | bytes 3145732 | tf_op jit(solution)/shard_map/while/body/jit(dynamic_update_index_in_dim)/dynamic_update_slice | solution.py:210
  288.2 8.8 fusion.207
  301.3 34.5 %dynamic_update_slice.63 = f32[4,256,24,64]{1,0,3,2:T(4,128)} dynamic-update-slice(f32[4,256,24,64]{1,0,3,2:T(4,128)} %get-tuple-element.1290, f32[1,256,24,64]{1,0,3,2:T(1,128)S(1)} %copy.348, s32[]{:T(128)} %get-tuple-element.1289, s32[]{:T(128)} %constant.337.clone.1..sunk.1, s32[]{:T(128)} %constant.337.clone.1..sunk.1, s32[]{:T(128)} %constant.337.clone.1..sunk.1) | dynamic-update-slice | bytes 3145732 | tf_op jit(solution)/shard_map/while/body/jit(dynamic_update_index_in_dim)/dynamic_update_slice | solution.py:210
  337.2 8.8 fusion.207
  350.2 34.5 %dynamic_update_slice.63 = f32[4,256,24,64]{1,0,3,2:T(4,128)} dynamic-update-slice(f32[4,256,24,64]{1,0,3,2:T(4,128)} %get-tuple-element.1290, f32[1,256,24,64]{1,0,3,2:T(1,128)S(1)} %copy.348, s32[]{:T(128)} %get-tuple-element.1289, s32[]{:T(128)} %constant.337.clone.1..sunk.1, s32[]{:T(128)} %constant.337.clone.1..sunk.1, s32[]{:T(128)} %constant.337.clone.1..sunk.1) | dynamic-update-slice | bytes 3145732 | tf_op jit(solution)/shard_map/while/body/jit(dynamic_update_index_in_dim)/dynamic_update_slice | solution.py:210
  386.2 8.8 fusion.207
  399.2 34.5 %dynamic_update_slice.63 = f32[4,256,24,64]{1,0,3,2:T(4,128)} dynamic-update-slice(f32[4,256,24,64]{1,0,3,2:T(4,128)} %get-tuple-element.1290, f32[1,256,24,64]{1,0,3,2:T(1,128)S(1)} %copy.348, s32[]{:T(128)} %get-tuple-element.1289, s32[]{:T(128)} %constant.337.clone.1..sunk.1, s32[]{:T(128)} %constant.337.clone.1..sunk.1, s32[]{:T(128)} %constant.337.clone.1..sunk.1) | dynamic-update-slice | bytes 3145732 | tf_op jit(solution)/shard_map/while/body/jit(dynamic_update_index_in_dim)/dynamic_update_slice | solution.py:210
  433.8 4.3 copy.310
  438.1 9.8 multiply_reduce_fusion.8
  448.0 7.7 multiply_reduce_fusion.5
  455.7 11.2 multiply_reduce_fusion.6
  466.9 8.2 reshape_reshape.7
  475.1 10.2 fusion.113
  487.5 9.1 while.96
  497.7 6.7 copy.248
  504.4 7.6 fusion.135
  512.1 92.7 %all-gather.16.cloned.1.call-done = f32[192,64,128]{2,1,0:T(8,128)} async-done(((f32[24,64,128]{2,1,0:T(8,128)}), f32[192,64,128]{2,1,0:T(8,128)}) %all-gather.16.cloned.1.call-update) | async-done | bytes 6291472 | tf_op jit(solution)/shard_map/all_gather | solution.py:23
  605.0 14.7 %while.93 = (s32[]{:T(128)}, f32[24,64,128]{2,1,0:T(8,128)S(1)}, s32[]{:T(128)}, f32[8,24]{1,0:T(8,128)}, f32[8,24,64,128]{3,2,1,0:T(8,128)}, /*index=5*/s32[]{:T(128)}, s32[]{:T(128)}, s32[]{:T(128)}, s32[]{:T(128)}) while((s32[]{:T(128)}, f32[24,64,128]{2,1,0:T(8,128)S(1)}, s32[]{:T(128)}, f32[8,24]{1,0:T(8,128)}, ...), condition=%wide.region_16.17_spmd, body=%wide.region_15.16_spmd.sunk | while | flops 393222 | bytes 2359731 | solution.py:32
  619.7 4.9 multiply_reduce_fusion.9
  628.7 306.9 %while.94 = (s32[]{:T(128)}, f32[4,256,24,64]{1,0,3,2:T(4,128)}, f32[4,256,128]{2,1,0:T(8,128)S(1)}, f32[4,256,128]{2,1,0:T(8,128)}, f32[4,256,24]{1,0,2:T(4,128...) while((s32[]{:T(128)}, f32[4,256,24,64]{1,0,3,2:T(4,128)}, ...), condition=%wide.region_28.29_spmd, body=%wide.region_18.28_spmd.sunk | while | flops 5167753216 | bytes 29749996 | solution.py:242
  634.0 11.4 fusion.225
  656.5 7.0 fusion.223
  665.2 34.5 %dynamic_update_slice.66 = f32[4,256,24,64]{1,0,3,2:T(4,128)} dynamic-update-slice(f32[4,256,24,64]{1,0,3,2:T(4,128)} %get-tuple-element.1381, f32[1,256,24,64]{1,0,3,2:T(1,128)S(1)} %copy.351, s32[]{:T(128)} %get-tuple-element.1380, s32[]{:T(128)} %constant.337.clone.1..sunk.3, s32[]{:T(128)} %constant.337.clone.1..sunk.3, s32[]{:T(128)} %constant.337.clone.1..sunk.3) | dynamic-update-slice | bytes 3145732 | tf_op jit(solution)/shard_map/while/body/jit(dynamic_update_index_in_dim)/dynamic_update_slice | solution.py:210
  710.6 11.4 fusion.225
  726.9 4.2 fusion.228
  733.0 7.0 fusion.223
  741.7 34.5 %dynamic_update_slice.66 = f32[4,256,24,64]{1,0,3,2:T(4,128)} dynamic-update-slice(f32[4,256,24,64]{1,0,3,2:T(4,128)} %get-tuple-element.1381, f32[1,256,24,64]{1,0,3,2:T(1,128)S(1)} %copy.351, s32[]{:T(128)} %get-tuple-element.1380, s32[]{:T(128)} %constant.337.clone.1..sunk.3, s32[]{:T(128)} %constant.337.clone.1..sunk.3, s32[]{:T(128)} %constant.337.clone.1..sunk.3) | dynamic-update-slice | bytes 3145732 | tf_op jit(solution)/shard_map/while/body/jit(dynamic_update_index_in_dim)/dynamic_update_slice | solution.py:210
  787.2 11.4 fusion.225
  809.6 7.0 fusion.223
  818.3 34.5 %dynamic_update_slice.66 = f32[4,256,24,64]{1,0,3,2:T(4,128)} dynamic-update-slice(f32[4,256,24,64]{1,0,3,2:T(4,128)} %get-tuple-element.1381, f32[1,256,24,64]{1,0,3,2:T(1,128)S(1)} %copy.351, s32[]{:T(128)} %get-tuple-element.1380, s32[]{:T(128)} %constant.337.clone.1..sunk.3, s32[]{:T(128)} %constant.337.clone.1..sunk.3, s32[]{:T(128)} %constant.337.clone.1..sunk.3) | dynamic-update-slice | bytes 3145732 | tf_op jit(solution)/shard_map/while/body/jit(dynamic_update_index_in_dim)/dynamic_update_slice | solution.py:210
  863.7 11.4 fusion.225
  886.2 7.0 fusion.223
  894.9 34.5 %dynamic_update_slice.66 = f32[4,256,24,64]{1,0,3,2:T(4,128)} dynamic-update-slice(f32[4,256,24,64]{1,0,3,2:T(4,128)} %get-tuple-element.1381, f32[1,256,24,64]{1,0,3,2:T(1,128)S(1)} %copy.351, s32[]{:T(128)} %get-tuple-element.1380, s32[]{:T(128)} %constant.337.clone.1..sunk.3, s32[]{:T(128)} %constant.337.clone.1..sunk.3, s32[]{:T(128)} %constant.337.clone.1..sunk.3) | dynamic-update-slice | bytes 3145732 | tf_op jit(solution)/shard_map/while/body/jit(dynamic_update_index_in_dim)/dynamic_update_slice | solution.py:210
  935.6 7.0 copy.311
  943.1 8.2 multiply_add_fusion.2
  951.5 13.1 multiply_reduce_fusion.4
  965.1 4.5 scatter-add.15
  970.0 4.6 multiply_add_fusion
  974.6 38.0 %scatter-add.16 = f32[1027,1792]{0,1:T(8,128)} dynamic-update-slice(f32[1027,1792]{0,1:T(8,128)} %scatter-add.15, f32[1024,1792]{0,1:T(8,128)} %multiply_add_fusion, s32[]{:T(128)} %constant.346.clone.1, s32[]{:T(128)} %constant.337.clone.1) | dynamic-update-slice | bytes 14680068 | tf_op jit(solution)/shard_map/scatter-add | solution.py:283
  1012.6 8.7 slice_add_fusion.2
  1021.3 38.0 %scatter-add.17 = f32[1027,1792]{0,1:T(8,128)} dynamic-update-slice(f32[1027,1792]{0,1:T(8,128)} %scatter-add.16, f32[1024,1792]{0,1:T(8,128)} %slice_add_fusion.2, s32[]{:T(128)} %constant.347.clone.1, s32[]{:T(128)} %constant.337.clone.1) | dynamic-update-slice | bytes 14680068 | tf_op jit(solution)/shard_map/scatter-add | solution.py:283
  1067.0 7.7 fusion.104
  1076.7 13.9 %fusion.131 = f32[768,3352]{1,0:T(8,128)} fusion(bf16[1024,24]{0,1:T(8,128)(2,1)S(1)} %get-tuple-element.906, bf16[1024,1792]{0,1:T(8,128)(2,1)S(1)} %fusion.104, bf16[1024,1536]{0,1:T(8,128)(2,1)S(1)} %copy-done.14, bf16[1,1024,768]{2,1,0:T(8,128)(2,1)S(1)} %copy-done.9, f32[768]{0:T(1024)S(1)} %copy-done.42, f32[1024]{0:T(1024)S(1)} %copy-done.37), kind=kOutput, calls=%fused_computation.203 | convolution fusion | flops 5295980544 | bytes 18742272 | tf_op jit(solution)/shard_map/td,tk->dk/dot_general | solution.py:293
  1092.4 81.7 %reduce-scatter.6.cloned.1.call-done = f32[192,3352]{1,0:T(8,128)} async-done(((f32[768,3352]{1,0:T(8,128)}), f32[192,3352]{1,0:T(8,128)}) %reduce-scatter.6.cloned.1.call-update) | async-done | bytes 2574352 | tf_op jit(solution)/shard_map/reduce_scatter | solution.py:306
  1177.0 7.7 fusion.139
  1184.7 10.8 fusion.127
  1195.5 10.8 all-reduce.16
  1211.3 39.9 %all-reduce.14 = (f32[448,4]{0,1:T(4,128)}, f32[448]{0:T(512)}, f32[6]{0:T(128)}, f32[6]{0:T(128)}, f32[6]{0:T(128)}, /*index=5*/f32[192]{0:T(256)}, f32[384]{0:T(512)}) all-reduce(f32[448,4]{0,1:T(4,128)S(1)} %copy.272, f32[448]{0:T(512)S(1)} %dynamic-slice.47, f32[6]{0:T(128)S(1)} %dynamic-slice.49, ...), channel_id=1, replica_groups=mesh['seq'=8,'fsdp'=4] {'seq'}, use_global_device_ids=true, to_apply=%region_39.40 | all-reduce | flops 2834 | bytes 22672 | tf_op jit(solution)/shard_map/psum | solution.py:316
  1251.2 101.9 %all-reduce.20.cloned.1.call-done = (f32[192,3352]{1,0:T(8,128)}, f32[384,768]{1,0:T(8,128)}) async-done(((f32[192,3352]{1,0:T(8,128)}, f32[384,768]{1,0:T(8,128)}), (f32[192,3352]{1,0:T(8,128)}, f32[384,768]{1,0:T(8,128)})) %all-reduce.20.cloned.1.call-update) | async-done | bytes 3754000 | tf_op jit(solution)/shard_map/psum | solution.py:316
  (416 shorter events, 218.4 us)
Async XLA Ops:
  7.2 46.1 %all-gather.10.cloned.1.call-start = ((), (), s32[]{:S(2)}) async-start(), calls=%async_computation.3 | async-start | bytes 6635520 | tf_op jit(solution)/shard_map/all_gather | solution.py:146
  7.9 221.4 %all-gather.14.cloned.1.call-start = ((), (), s32[]{:S(2)}) async-start(), calls=%async_computation.7 | async-start | bytes 7077888 | tf_op jit(solution)/shard_map/all_gather | solution.py:23
  24.0 7.4 copy-start.52
  24.0 38.2 %copy-start.41 = (f32[768]{0:T(1024)}, f32[768]{0:T(1024)S(1)}, u32[]{:S(2)}) copy-start(f32[768]{0:T(1024)S(1)} %convert_element_type.67) | copy-start | bytes 9220
  24.1 38.4 %copy-start.47 = (f32[24]{0:T(128)}, f32[24]{0:T(128)S(1)}, u32[]{:S(2)}) copy-start(f32[24]{0:T(128)S(1)} %convert_element_type.72) | copy-start | bytes 292
  29.6 54.8 %copy-start.22 = (f32[1792]{0:T(1024)}, f32[1792]{0:T(1024)S(1)}, u32[]{:S(2)}) copy-start(f32[1792]{0:T(1024)S(1)} %get-tuple-element.789) | copy-start | bytes 21508
  29.7 54.8 %copy-start.24 = (f32[1792]{0:T(1024)}, f32[1792]{0:T(1024)S(1)}, u32[]{:S(2)}) copy-start(f32[1792]{0:T(1024)S(1)} %get-tuple-element.790) | copy-start | bytes 21508
  29.7 54.8 %copy-start.26 = (f32[1792]{0:T(1024)}, f32[1792]{0:T(1024)S(1)}, u32[]{:S(2)}) copy-start(f32[1792]{0:T(1024)S(1)} %get-tuple-element.788) | copy-start | bytes 21508
  29.7 54.8 %copy-start.28 = (f32[1792]{0:T(1024)}, f32[1792]{0:T(1024)S(1)}, u32[]{:S(2)}) copy-start(f32[1792]{0:T(1024)S(1)} %get-tuple-element.787) | copy-start | bytes 21508
  31.5 31.0 %copy-start.49 = (f32[24]{0:T(128)}, f32[24]{0:T(128)S(1)}, u32[]{:S(2)}) copy-start(f32[24]{0:T(128)S(1)} %exponential_negate_fusion) | copy-start | bytes 292
  32.1 30.2 %copy-start.36 = (f32[1024]{0:T(1024)}, f32[1024]{0:T(1024)S(1)}, u32[]{:S(2)}) copy-start(f32[1024]{0:T(1024)S(1)} %get-tuple-element.927) | copy-start | bytes 12292
  67.8 14.2 %slice-start.2 = ((bf16[1024,3352]{0,1:T(8,128)(2,1)}), bf16[1024,1792]{0,1:T(8,128)(2,1)S(1)}, s32[]{:S(2)}) async-start(bf16[1024,3352]{0,1:T(8,128)(2,1)} %copy-done.8), calls=%async_computation.13 | async-start | bytes 7340032 | tf_op jit(solution)/shard_map/slice | solution.py:176
  68.1 13.8 %collective-permute-start = (bf16[3,1792]{0,1:T(8,128)(2,1)S(1)}, bf16[3,1792]{0,1:T(8,128)(2,1)S(1)}, u32[]{:S(2)}, u32[]{:S(2)}) collective-permute-start(bf16[3,1792]{0,1:T(8,128)(2,1)S(1)} %slice.203), channel_id=1, source_target_pairs={{0,4},{4,8},{8,12},{12,16},{16,20},{20,24},{24,28},{1,5},{5,9},{9,... | collective-permute-start | bytes 32264 | tf_op jit(solution)/shard_map/ppermute | solution.py:16
  84.4 9.1 copy-start
  93.4 4.8 copy-start.2
  118.8 10.8 copy-start.54
  118.8 11.5 copy-start.51
  128.8 319.2 %all-gather.12.cloned.1.call-start = ((), (), s32[]{:S(2)}) async-start(), calls=%async_computation.4 | async-start | bytes 2949120 | tf_op jit(solution)/shard_map/all_gather | solution.py:147
  129.5 475.4 %all-gather.16.cloned.1.call-start = ((), (), s32[]{:S(2)}) async-start(), calls=%async_computation.8 | async-start | bytes 7077888 | tf_op jit(solution)/shard_map/all_gather | solution.py:23
  135.5 368.9 %copy-start.30 = (f32[1536]{0:T(1024)}, f32[1536]{0:T(1024)S(1)}, u32[]{:S(2)}) copy-start(f32[1536]{0:T(1024)S(1)} %reshape.457) | copy-start | bytes 18436
  160.1 69.7 %copy-start.33 = (f32[4,24]{1,0:T(4,128)}, f32[4,24]{1,0:T(4,128)S(1)}, u32[]{:S(2)}) copy-start(f32[4,24]{1,0:T(4,128)S(1)} %get-tuple-element.931) | copy-start | bytes 1156
  168.0 61.4 %copy-start.10 = (f32[4,256,128]{1,0,2:T(4,128)}, f32[4,256,128]{1,0,2:T(4,128)S(1)}, u32[]{:S(2)}) copy-start(f32[4,256,128]{1,0,2:T(4,128)S(1)} %reshape.418) | copy-start | bytes 1572868
  229.8 8.0 copy-start.46
  438.1 9.8 copy-start.5
  438.1 9.9 copy-start.16
  447.9 7.8 copy-start.38
  448.0 7.7 copy-start.6
  448.0 7.7 copy-start.7
  466.9 8.2 copy-start.11
  497.6 594.8 %reduce-scatter.8.cloned.1.call-start = ((), (), s32[]{:S(2)}) async-start(), calls=%async_computation.6 | async-start | bytes 5898240 | tf_op jit(solution)/shard_map/reduce_scatter | solution.py:307
  497.7 6.8 copy-start.17
  497.7 6.7 copy-start.39
  512.1 662.0 %reduce-scatter.6.cloned.1.call-start = ((), (), s32[]{:S(2)}) async-start(), calls=%async_computation.5 | async-start | bytes 13271040 | tf_op jit(solution)/shard_map/reduce_scatter | solution.py:306
  604.9 14.8 %copy-start.34 = (f32[4,24]{1,0:T(4,128)S(1)}, f32[4,24]{1,0:T(4,128)}, u32[]{:S(2)}) copy-start(f32[4,24]{1,0:T(4,128)} %copy-done.33) | copy-start | bytes 1156
  604.9 14.8 %copy-start.43 = (f32[4,24]{1,0:T(4,128)S(1)}, f32[4,24]{1,0:T(4,128)}, u32[]{:S(2)}) copy-start(f32[4,24]{1,0:T(4,128)} %get-tuple-element.930) | copy-start | bytes 1156
  604.9 14.8 %copy-start.44 = (f32[4,24]{1,0:T(4,128)S(1)}, f32[4,24]{1,0:T(4,128)}, u32[]{:S(2)}) copy-start(f32[4,24]{1,0:T(4,128)} %get-tuple-element.932) | copy-start | bytes 1156
  624.6 4.1 copy-start.19
  624.6 4.1 copy-start.21
  935.6 7.2 copy-start.20
  943.0 8.2 slice-start
  943.1 8.4 slice-start.1
  951.5 13.1 copy-start.29
  964.6 5.5 copy-start.1
  965.1 4.9 copy-start.25
  974.6 38.0 %copy-start.23 = (f32[1792]{0:T(1024)S(1)}, f32[1792]{0:T(1024)}, u32[]{:S(2)}) copy-start(f32[1792]{0:T(1024)} %copy-done.22) | copy-start | bytes 21508
  1021.3 40.9 %copy-start.48 = (f32[24]{0:T(128)S(1)}, f32[24]{0:T(128)}, u32[]{:S(2)}) copy-start(f32[24]{0:T(128)} %copy-done.47) | copy-start | bytes 292
  1021.3 40.9 %copy-start.50 = (f32[24]{0:T(128)S(1)}, f32[24]{0:T(128)}, u32[]{:S(2)}) copy-start(f32[24]{0:T(128)} %copy-done.49) | copy-start | bytes 292
  1021.3 45.7 %copy-start.27 = (f32[1792]{0:T(1024)S(1)}, f32[1792]{0:T(1024)}, u32[]{:S(2)}) copy-start(f32[1792]{0:T(1024)} %copy-done.26) | copy-start | bytes 21508
  1060.9 5.8 collective-permute-start.1
  1067.0 9.7 copy-start.9
  1067.0 9.7 copy-start.14
  1067.0 9.7 copy-start.37
  1067.0 9.7 copy-start.42
  1090.6 86.1 %copy-start.32 = (f32[1536]{0:T(1024)S(1)}, f32[1536]{0:T(1024)}, u32[]{:S(2)}) copy-start(f32[1536]{0:T(1024)} %get-tuple-element.903) | copy-start | bytes 18436
  1090.6 86.3 %copy-start.31 = (f32[1536]{0:T(1024)S(1)}, f32[1536]{0:T(1024)}, u32[]{:S(2)}) copy-start(f32[1536]{0:T(1024)} %copy-done.30) | copy-start | bytes 18436
  1090.6 86.3 %copy-start.40 = (f32[1024]{0:T(1024)S(1)}, f32[1024]{0:T(1024)}, u32[]{:S(2)}) copy-start(f32[1024]{0:T(1024)} %copy-done.38) | copy-start | bytes 12292
  1090.6 119.5 %reduce-scatter.10.cloned.1.call-start = ((), (), s32[]{:S(2)}) async-start(), calls=%async_computation.9 | async-start | bytes 1146880
  1092.1 261.0 %all-reduce.20.cloned.1.call-start = ((), (), s32[]{:S(2)}) async-start(), calls=%async_computation.10 | async-start | bytes 7667712 | tf_op jit(solution)/shard_map/psum | solution.py:316
  1177.0 7.7 copy-start.53
  1177.0 7.7 copy-start.13
  1177.0 7.7 copy-start.15
  1184.7 10.8 copy-start.45
  1184.7 22.1 %copy-start.18 = (bf16[1,1024,768]{2,1,0:T(8,128)(2,1)S(1)}, bf16[1,1024,768]{2,1,0:T(8,128)(2,1)}, u32[]{:S(2)}) copy-start(bf16[1,1024,768]{2,1,0:T(8,128)(2,1)} %param.43) | copy-start | bytes 4718596
  1184.7 22.1 %copy-start.35 = (f32[1024]{0:T(1024)S(1)}, f32[1024]{0:T(1024)}, u32[]{:S(2)}) copy-start(f32[1024]{0:T(1024)} %get-tuple-element.926) | copy-start | bytes 12292
  (4 other events, 6.5 us)
Sparse Core Ops, SparseCore 0:
  9.6 43.6 all-gather.9
  128.9 100.3 all-gather.13
  230.9 22.2 all-gather.11
  497.7 107.1 all-gather.15
  607.3 46.0 reduce-scatter.7
  1090.8 83.3 reduce-scatter.5
  1177.4 24.2 reduce-scatter.9
  1205.4 147.6 all-reduce.19
where the time goes:
time: 1380 us; the launch traced here: 1370 us
  local copies, waits for them, and re-layouts  466 us (34%)
  waiting for transfers between devices  372 us (27%)
  matrix products  279 us (20%)
  other arithmetic  127 us (9%)
  blocking collectives  92.6 us (7%)
  between operations  20.6 us (1%)
    dynamic_update_slice x16, local copies, waits for them, and re-layouts, on_device(): lax.map(span_forward, (span_values, span_write, span_read, span_step, cum...  289 us
    all_gather x2, waiting for transfers between devices, prefix(): gathered = jax.tree.map(lambda a: lax.all_gather(a, axis), part)  153 us
    psum x1, waiting for transfers between devices, on_device(): lax.psum((parted[0], parted[1], parted[2], parted[3], parted[4], parted[5...  102 us
    reduce_scatter x1, waiting for transfers between devices, on_device(): lax.psum_scatter(grad_inproj, 'fsdp', scatter_dimension=0, tiled=True)  81.7 us
    scatter-add x3, local copies, waits for them, and re-layouts, on_device(): grad_extended.at[tap_index:tap_index + length]  80.5 us
    dot_general x4, matrix products, span_backward(): jnp.einsum('thp,shp->tsh', grad_mixed, values, precision=highest)  45.6 us
    unnamed x3, blocking collectives  42.3 us
    psum x1, blocking collectives, on_device(): lax.psum((parted[0], parted[1], parted[2], parted[3], parted[4], parted[5...  39.9 us
  transfers between devices with their start and end apart: 10, of which 7 were waited for; matrix products, arithmetic and copies ran while one was open for 55% of the time, Pallas kernels for 0%

commit v1 on v0

v1 whole, which is shorter than its diff:
```python
import functools

import jax
import jax.numpy as jnp
from jax import lax
from jax.experimental import pallas as pl
from jax.experimental.pallas import tpu as pltpu
from jax.sharding import PartitionSpec as P

SPAN = 256
LANES = 128

epsilon = 1e-05
highest = lax.Precision.HIGHEST
f32 = jnp.float32
bf16 = jnp.bfloat16

NN = (((1,), (0,)), ((), ()))
NT = (((1,), (1,)), ((), ()))
TN = (((0,), (0,)), ((), ()))


def split(a):
    high = a.astype(bf16)
    return high, (a - high.astype(f32)).astype(bf16)


def mm3(a, b, dims):
    ah, al = a
    bh, bl = b
    dot = functools.partial(lax.dot_general, dimension_numbers=dims, preferred_element_type=f32)
    return dot(ah, bh) + (dot(ah, bl) + dot(al, bh))


def masked(pair, keep):
    return tuple(jnp.where(keep, part, jnp.zeros_like(part)) for part in pair)


def pick(lane_first, cols, a, b):
    return jnp.where(lane_first, cols[:, a : a + 1], cols[:, b : b + 1])


def forward_kernel(v_ref, w_ref, r_ref, rows_ref, first_ref, skip_ref, y_ref, ent_ref, state, scores):
    pair, chunk = pl.program_id(0), pl.program_id(1)
    w = split(w_ref[...])
    r = split(r_ref[...])

    @pl.when(pair == 0)
    def _():
        scores[chunk] = mm3(r, w, NT)

    @pl.when(chunk == 0)
    def _():
        state[...] = first_ref[...]

    rows = rows_ref[0, 0]
    cols = rows.T
    span = rows.shape[1]
    lane_first = lax.broadcasted_iota(jnp.int32, (1, LANES), 1) < LANES // 2
    causal = lax.broadcasted_iota(jnp.int32, (span, span), 0) >= lax.broadcasted_iota(
        jnp.int32, (span, span), 1
    )
    values = v_ref[...]
    v = split(values)
    held = state[...]
    ent_ref[0] = held
    scored = scores[chunk]
    total = pick(lane_first, cols, 0, 1)
    y = jnp.exp(total) * mm3(r, split(held), NN) + skip_ref[...] * values
    for head in range(2):
        gap = jnp.where(causal, cols[:, head : head + 1] - rows[head : head + 1], 0.0)
        weights = jnp.where(causal, jnp.exp(gap) * scored * rows[2 + head : 3 + head], 0.0)
        keep = lane_first if head == 0 else jnp.logical_not(lane_first)
        y = y + mm3(split(weights), masked(v, keep), NN)
    y_ref[...] = y
    last = total[span - 1 : span]
    tail = jnp.exp(last - total) * pick(lane_first, cols, 2, 3)
    state[...] = jnp.exp(last) * held + mm3(w, split(tail * values), TN)


def backward_kernel(
    v_ref, w_ref, r_ref, rows_ref, first_ref, skip_ref, ent_ref, gm_ref,
    gv_ref, gw_ref, gr_ref, out_ref,
    state, scores, score_grads,
):
    pair, lap = pl.program_id(0), pl.program_id(1)
    chunk = pl.num_programs(1) - 1 - lap
    w = split(w_ref[...])
    r = split(r_ref[...])
    rows = rows_ref[0, 0]
    cols = rows.T
    span = rows.shape[1]
    here = pl.ds(pl.multiple_of(chunk * span, span), span)

    @pl.when(pair == 0)
    def _():
        scores[chunk] = mm3(r, w, NT)
        score_grads[chunk] = jnp.zeros((span, span), f32)
        gw_ref[here, :] = jnp.zeros((span, LANES), f32)
        gr_ref[here, :] = jnp.zeros((span, LANES), f32)

    @pl.when(lap == 0)
    def _():
        state[...] = first_ref[...]

    lane = lax.broadcasted_iota(jnp.int32, (1, LANES), 1)
    lane_first = lane < LANES // 2
    causal = lax.broadcasted_iota(jnp.int32, (span, span), 0) >= lax.broadcasted_iota(
        jnp.int32, (span, span), 1
    )
    values = v_ref[...]
    v = split(values)
    grad_mixed = gm_ref[...]
    g = split(grad_mixed)
    entering = ent_ref[0]
    ent = split(entering)
    leaving = state[...]
    leav = split(leaving)
    scored = scores[chunk]
    total = pick(lane_first, cols, 0, 1)
    last = total[span - 1 : span]
    grown = jnp.exp(total) * grad_mixed
    gg = split(grown)
    fading = jnp.exp(last - total)
    tail = fading * pick(lane_first, cols, 2, 3)
    tv = split(tail * values)
    carried = grown * mm3(r, ent, NN)
    state_rows = mm3(w, leav, NN)
    ending = state_rows * values * fading
    grad_values = skip_ref[...] * grad_mixed + tail * state_rows
    joined = jnp.sum(leaving * (jnp.exp(last) * entering), axis=0, keepdims=True)
    back = jnp.zeros((span, LANES), f32)
    sums = []
    grads = score_grads[chunk]
    for head in range(2):
        keep = lane_first if head == 0 else jnp.logical_not(lane_first)
        gap = jnp.where(causal, cols[:, head : head + 1] - rows[head : head + 1], 0.0)
        kernel = jnp.where(causal, jnp.exp(gap), 0.0)
        step = rows[2 + head : 3 + head]
        gh = masked(g, keep)
        weights = split(scored * kernel * step)
        grad_values = grad_values + mm3(weights, gh, TN)
        shaped = mm3(gh, v, NT) * kernel
        grads = grads + shaped * step
        products = shaped * scored
        sums.append(jnp.sum(products, axis=0, keepdims=True))
        by_row = jnp.sum(products * step, axis=1, keepdims=True) + jnp.sum(
            jnp.where(keep, carried, 0.0), axis=1, keepdims=True
        )
        by_end = jnp.sum(jnp.where(keep, ending, 0.0), axis=1, keepdims=True)
        whole = jnp.sum(jnp.where(keep, joined, 0.0), axis=1, keepdims=True)
        back = jnp.where(lane == head, by_row, back)
        back = jnp.where(lane == 2 + head, by_end, back)
        back = jnp.where(lane == 6 + head, whole, back)
    score_grads[chunk] = grads
    gv_ref[...] = grad_values
    out_ref[0, 0] = back.T[:8]
    out_ref[0, 0, 4:5, :] = sums[0]
    out_ref[0, 0, 5:6, :] = sums[1]
    gr_ref[here, :] += mm3(gg, ent, NT)
    gw_ref[here, :] += mm3(tv, leav, NT)
    state[...] = mm3(r, gg, TN) + jnp.exp(last) * leaving

    @pl.when(pair == pl.num_programs(0) - 1)
    def _():
        s = split(grads)
        gr_ref[here, :] += mm3(s, w, NN)
        gw_ref[here, :] += mm3(s, r, TN)


def scan_forward(values, write_rows, read_rows, rows, first, skip_row):
    length, width = values.shape
    pairs, spans = rows.shape[0], rows.shape[1]
    states = first.shape[0]
    wide = pl.BlockSpec((SPAN, LANES), lambda p, c: (c, p))
    thin = pl.BlockSpec((SPAN, states), lambda p, c: (c, 0))
    return pl.pallas_call(
        forward_kernel,
        grid=(pairs, spans),
        in_specs=[
            wide, thin, thin,
            pl.BlockSpec((1, 1, 8, SPAN), lambda p, c: (p, c, 0, 0)),
            pl.BlockSpec((states, LANES), lambda p, c: (0, p)),
            pl.BlockSpec((1, LANES), lambda p, c: (0, p)),
        ],
        out_specs=[wide, pl.BlockSpec((1, states, LANES), lambda p, c: (c, 0, p))],
        out_shape=[
            jax.ShapeDtypeStruct((length, width), f32),
            jax.ShapeDtypeStruct((spans, states, width), f32),
        ],
        scratch_shapes=[pltpu.VMEM((states, LANES), f32), pltpu.VMEM((spans, SPAN, SPAN), f32)],
        compiler_params=pltpu.CompilerParams(vmem_limit_bytes=32 * 1024 * 1024),
        name="scan_forward",
    )(values, write_rows, read_rows, rows, first, skip_row)


def scan_backward(values, write_rows, read_rows, rows, first, skip_row, entering, grad_mixed):
    length, width = values.shape
    pairs, spans = rows.shape[0], rows.shape[1]
    states = first.shape[0]
    end = spans - 1
    wide = pl.BlockSpec((SPAN, LANES), lambda p, c: (end - c, p))
    thin = pl.BlockSpec((SPAN, states), lambda p, c: (end - c, 0))
    whole = pl.BlockSpec((length, states), lambda p, c: (0, 0))
    lines = pl.BlockSpec((1, 1, 8, SPAN), lambda p, c: (p, end - c, 0, 0))
    return pl.pallas_call(
        backward_kernel,
        grid=(pairs, spans),
        in_specs=[
            wide, thin, thin, lines,
            pl.BlockSpec((states, LANES), lambda p, c: (0, p)),
            pl.BlockSpec((1, LANES), lambda p, c: (0, p)),
            pl.BlockSpec((1, states, LANES), lambda p, c: (end - c, 0, p)),
            wide,
        ],
        out_specs=[wide, whole, whole, lines],
        out_shape=[
            jax.ShapeDtypeStruct((length, width), f32),
            jax.ShapeDtypeStruct((length, states), f32),
            jax.ShapeDtypeStruct((length, states), f32),
            jax.ShapeDtypeStruct((pairs, spans, 8, SPAN), f32),
        ],
        scratch_shapes=[
            pltpu.VMEM((states, LANES), f32),
            pltpu.VMEM((spans, SPAN, SPAN), f32),
            pltpu.VMEM((spans, SPAN, SPAN), f32),
        ],
        compiler_params=pltpu.CompilerParams(vmem_limit_bytes=32 * 1024 * 1024),
        name="scan_backward",
    )(values, write_rows, read_rows, rows, first, skip_row, entering, grad_mixed)


def from_behind(array, axis, by):
    devices = lax.axis_size(axis)
    pairs = [(i, i + by) for i in range(devices) if 0 <= i + by < devices]
    return lax.ppermute(array, axis, pairs)


def swap(array, axis):
    return lax.all_to_all(array, axis, 0, 0, tiled=True)


def prefix(part, logs, widen, reverse):
    count = logs.shape[0]
    states, width = part.shape
    parts = swap(part, "seq").reshape(count, states // count, width)
    ends = jnp.cumsum(logs, axis=0)
    place = jnp.arange(count)
    if reverse:
        used = place[None, :] > place[:, None]
        gaps = (ends - logs)[None, :] - ends[:, None]
    else:
        used = place[None, :] < place[:, None]
        gaps = (ends - logs)[:, None] - ends[None, :]
    used = used[:, :, None]
    factors = jnp.where(used, jnp.exp(jnp.where(used, gaps, 0.0)), 0.0)
    factors = widen(factors.reshape(count * count, -1)).reshape(count, count, 1, width)
    total = jnp.sum(factors * parts[None], axis=1)
    return swap(total.reshape(states, width), "seq")


def gather_sum(grad):
    owners = lax.axis_size("fsdp")
    pieces = lax.axis_size("seq")
    rows, width = grad.shape
    share = swap(grad.astype(bf16), "fsdp").reshape(owners, rows // owners, width)
    share = jnp.sum(share.astype(f32), axis=0)
    parts = swap(share.astype(bf16), "seq").reshape(pieces, rows // owners // pieces, width)
    part = jnp.sum(parts.astype(f32), axis=0)
    return lax.all_gather(part, "seq", axis=0, tiled=True)


def plain_sum(grad):
    share = lax.psum_scatter(grad, "fsdp", scatter_dimension=0, tiled=True)
    return lax.psum(share, "seq")


def silu_slope(inputs):
    sig_value = jax.nn.sigmoid(inputs)
    return sig_value * (1.0 + inputs * (1.0 - sig_value))


def on_device(
    tokens, in_weight, out_weight, conv_weight, conv_bias, step_bias,
    decay_param, skip_gain, norm_gain, gate_gain, cotangent,
):
    smalls = (conv_weight.reshape(-1), conv_bias, step_bias, decay_param, skip_gain, norm_gain, gate_gain)
    sizes = [a.shape[0] for a in smalls]
    offsets = [sum(sizes[:i]) for i in range(len(sizes) + 1)]
    packed = lax.all_gather(jnp.concatenate(smalls)[None], "fsdp", axis=0, tiled=True).astype(f32)
    full = [packed[:, offsets[i] : offsets[i + 1]].reshape(-1) for i in range(len(sizes))]
    tap_count = conv_weight.shape[1]
    conv_taps = full[0].reshape(-1, tap_count)
    conv_offset, step_offset, decay_values, skip_values, gain_in, gain_out = full[1:]
    full_in = lax.all_gather(in_weight, "fsdp", axis=0, tiled=True)
    full_out = lax.all_gather(out_weight, "fsdp", axis=0, tiled=True)
    length = tokens.shape[1]
    head_count = step_offset.shape[0]
    inner_width = full_out.shape[0]
    conv_width = conv_taps.shape[0]
    state_dim = (conv_width - inner_width) // 2
    head_dim = inner_width // head_count
    span_count = length // SPAN
    pairs = head_count // 2
    spread = (jnp.arange(inner_width)[None, :] // head_dim == jnp.arange(head_count)[:, None]).astype(f32)

    def widen(a):
        return jnp.dot(a, spread, precision=highest)

    source = tokens[0].astype(f32)
    in_scale = lax.rsqrt(jnp.mean(source * source, axis=1, keepdims=True) + epsilon)
    normed = (source * in_scale * gain_in).astype(bf16)
    projected = jnp.dot(normed, full_in, preferred_element_type=f32).astype(bf16)
    gate_part = projected[:, :inner_width].astype(f32)
    conv_in = projected[:, inner_width : inner_width + conv_width]
    step_raw = projected[:, inner_width + conv_width :].astype(f32)
    rim = tap_count - 1
    rim_rows = from_behind(conv_in[length - rim :], "seq", 1)
    lead = 16
    extended = jnp.concatenate(
        [jnp.zeros((lead - rim, conv_width), bf16), rim_rows, conv_in], axis=0
    ).astype(f32)
    shifted = [extended[lead - rim + k : lead - rim + k + length] for k in range(tap_count)]
    conv_sum = conv_offset[None, :] + sum(conv_taps[:, k] * shifted[k] for k in range(tap_count))
    conv_out = jax.nn.silu(conv_sum)
    values = conv_out[:, :inner_width]
    write_rows = conv_out[:, inner_width : inner_width + state_dim]
    read_rows = conv_out[:, inner_width + state_dim :]
    step_pre = step_raw + step_offset
    dt_step = jax.nn.softplus(step_pre)
    decay_rate = -jnp.exp(decay_values)
    decay_log = dt_step * decay_rate
    cumulative = jnp.cumsum(decay_log.reshape(span_count, SPAN, head_count), axis=1)
    span_log = cumulative[:, -1]
    prior_log = jnp.cumsum(span_log, axis=0) - span_log
    device_log = jnp.sum(span_log, axis=0)
    along = (cumulative + prior_log[:, None, :]).reshape(length, head_count)
    logs = lax.all_gather(device_log, "seq")

    def as_rows(a):
        return a.reshape(span_count, SPAN, pairs, 2).transpose(2, 0, 3, 1)

    step_rows = as_rows(dt_step)
    rows = jnp.concatenate(
        [as_rows(cumulative), step_rows, jnp.zeros((pairs, span_count, 4, SPAN), f32)], axis=2
    )
    skip_row = widen(skip_values[None])
    tail = widen(jnp.exp(device_log[None, :] - along) * dt_step)
    final_local = lax.dot_general(write_rows, tail * values, TN, precision=highest)
    incoming = prefix(final_local, logs, widen, False)
    flat, entering = scan_forward(values, write_rows, read_rows, rows, incoming, skip_row)
    gate_silu = jax.nn.silu(gate_part)
    gated = flat * gate_silu
    gate_scale = lax.rsqrt(jnp.mean(gated * gated, axis=1, keepdims=True) + epsilon)
    normed_out = (gated * gate_scale * gain_out).astype(bf16)
    block_out = source + jnp.dot(normed_out, full_out, preferred_element_type=f32)
    grad_out = cotangent[0]
    grad_outproj = jnp.einsum("ti,td->id", normed_out, grad_out, preferred_element_type=f32)
    grad_normed = jnp.einsum("td,id->ti", grad_out, full_out, preferred_element_type=f32)
    grad_gategain = jnp.sum(grad_normed * gated * gate_scale, axis=0)
    grad_scaled = grad_normed * gain_out
    grad_gated = gate_scale * grad_scaled - gated * gate_scale**3 * jnp.mean(
        grad_scaled * gated, axis=1, keepdims=True
    )
    grad_gate = (grad_gated * flat * silu_slope(gate_part)).astype(bf16)
    grad_mixed = grad_gated * gate_silu
    grad_skip = jnp.sum(jnp.sum(grad_mixed * values, axis=0).reshape(head_count, head_dim), axis=1)
    start_grad = lax.dot_general(read_rows, widen(jnp.exp(along)) * grad_mixed, TN, precision=highest)
    outgoing = prefix(start_grad, logs, widen, True)
    grad_outproj = plain_sum(grad_outproj)
    grad_gateproj = plain_sum(
        jnp.einsum("td,tk->dk", normed, grad_gate, preferred_element_type=f32)
    )
    grad_values, grad_write, grad_read, back = scan_backward(
        values, write_rows, read_rows, rows, outgoing, skip_row, entering, grad_mixed
    )
    flowing = jnp.sum(back[:, :, 2:4] * step_rows, axis=3)
    grad_cumul = back[:, :, 0:2] - step_rows * (back[:, :, 2:4] + back[:, :, 4:6])
    behind = jnp.sum(grad_cumul, axis=3, keepdims=True) - jnp.cumsum(grad_cumul, axis=3) + grad_cumul
    grad_log = behind + (flowing + back[:, :, 6:8, 0])[..., None]

    def from_rows(a):
        return a.transpose(1, 3, 0, 2).reshape(length, head_count)

    grad_decaylog = from_rows(grad_log)
    grad_step = from_rows(back[:, :, 2:4] + back[:, :, 4:6]) + grad_decaylog * decay_rate
    grad_decay = jnp.sum(grad_decaylog * dt_step, axis=0) * decay_rate
    grad_pre = grad_step * jax.nn.sigmoid(step_pre)
    grad_stepbias = jnp.sum(grad_pre, axis=0)
    grad_sum = jnp.concatenate([grad_values, grad_write, grad_read], axis=1) * silu_slope(conv_sum)
    grad_convbias = jnp.sum(grad_sum, axis=0)
    grad_conv = jnp.stack([jnp.sum(grad_sum * shifted[k], axis=0) for k in range(tap_count)], axis=1)
    next_rows = from_behind(grad_sum[:rim], "seq", -1)
    reaching = jnp.concatenate([grad_sum, next_rows], axis=0)
    grad_conv_in = sum(conv_taps[:, k] * reaching[rim - k : rim - k + length] for k in range(tap_count))
    grad_rest = jnp.concatenate([grad_conv_in, grad_pre], axis=1).astype(bf16)
    grad_restproj = jnp.einsum("td,tk->dk", normed, grad_rest, preferred_element_type=f32)
    grad_normed_in = jnp.einsum(
        "tk,dk->td", grad_gate, full_in[:, :inner_width], preferred_element_type=f32
    ) + jnp.einsum("tk,dk->td", grad_rest, full_in[:, inner_width:], preferred_element_type=f32)
    grad_normgain = jnp.sum(grad_normed_in * source * in_scale, axis=0)
    grad_scaled_in = grad_normed_in * gain_in
    grad_source = in_scale * grad_scaled_in - source * in_scale**3 * jnp.mean(
        grad_scaled_in * source, axis=1, keepdims=True
    )
    grad_source = grad_source + grad_out.astype(f32)
    owners = lax.axis_size("fsdp")
    small_grads = (
        grad_conv.reshape(-1), grad_convbias, grad_stepbias, grad_decay,
        grad_skip, grad_normgain, grad_gategain,
    )
    small = jnp.concatenate([a.reshape(owners, -1) for a in small_grads], axis=1)
    small = lax.psum(small, ("fsdp", "seq"))
    mine = lax.dynamic_index_in_dim(small, lax.axis_index("fsdp"), 0, False)
    shares = [mine[offsets[i] : offsets[i + 1]] for i in range(len(sizes))]
    grad_inproj = jnp.concatenate([grad_gateproj, gather_sum(grad_restproj)], axis=1)
    return (
        block_out[None].astype(bf16),
        grad_source[None].astype(bf16),
        grad_inproj,
        grad_outproj,
        shares[0].reshape(-1, tap_count),
        *shares[1:],
    )


def solution(mesh):
    placed = (
        P("fsdp", "seq", None),
        P("fsdp", None),
        P("fsdp", None),
        P("fsdp", None),
        P("fsdp"),
        P("fsdp"),
        P("fsdp"),
        P("fsdp"),
        P("fsdp"),
        P("fsdp"),
        P("fsdp", "seq", None),
    )
    return jax.shard_map(
        on_device,
        mesh=mesh,
        in_specs=placed,
        out_specs=(
            P("fsdp", "seq", None),
            P("fsdp", "seq", None),
            P("fsdp", None),
            P("fsdp", None),
            P("fsdp", None),
            P("fsdp"),
            P("fsdp"),
            P("fsdp"),
            P("fsdp"),
            P("fsdp"),
            P("fsdp"),
        ),
        check_vma=False,
    )
```

time: 1380 us -> 674 us (0.49)
  local copies, waits for them, and re-layouts: 466 us -> 71.1 us
  waiting for transfers between devices: 372 us -> 144 us
  matrix products: 279 us -> 84.3 us
  Pallas kernels: 0 us -> 108 us
  blocking collectives: 92.6 us -> 141 us
  other arithmetic: 127 us -> 80.1 us
  starting transfers between devices: 5.71 us -> 22.1 us
    dynamic_update_slice x32 -> x0, local copies, waits for them, and re-layouts: 291 us -> none  [the longest x16 289 us: on_device(): lax.map(span_forward, (span_values, span_write, span_read, span_step, cum...]
    dot_general x56 -> x15, matrix products: 279 us -> 84.3 us  [the longest x1 9.46 us: on_device(): jnp.einsum('tk,dk->td', grad_rest, full_in[:, inner_width:], preferred_el...]
    all_gather x4 -> x3, waiting for transfers between devices: 174 us -> 20.3 us  [the longest x1 20.2 us: on_device(): full_in = lax.all_gather(in_weight, 'fsdp', axis=0, tiled=True)]
    pallas_call x0 -> x2, Pallas kernels: none -> 108 us  [the longest x1 66.4 us: scan_backward(): pl.pallas_call(backward_kernel, grid=(pairs, spans), in_specs=[wide, thin...]
    reduce_scatter x2, waiting for transfers between devices: 81.7 us -> 0.01 us  [plain_sum(): share = lax.psum_scatter(grad, 'fsdp', scatter_dimension=0, tiled=True)]
    scatter-add x7 -> x0, local copies, waits for them, and re-layouts: 80.9 us -> none  [the longest x3 80.5 us: on_device(): grad_extended.at[tap_index:tap_index + length]]
    all_to_all x0 -> x2, blocking collectives: none -> 62.6 us  [swap(): return lax.all_to_all(array, axis, 0, 0, tiled=True)]
    add x27 -> x2, other arithmetic: 45.8 us -> 1.07 us  [the longest x1 0.97 us: on_device(): grad_log = behind + (flowing + back[:, :, 6:8, 0])[..., None]]
  transfers between devices with their start and end apart: 10 -> 12, of which waited for: 7 -> 6; matrix products, arithmetic and copies ran while one was open for 55% -> 21% of each run, Pallas kernels for 0% -> 16%
where the time goes in v1:
time: 674 us; the launch traced here: 667 us
  waiting for transfers between devices  144 us (21%)
  blocking collectives  141 us (21%)
  Pallas kernels  108 us (16%)
  matrix products  84.3 us (13%)
  other arithmetic  80.1 us (12%)
  local copies, waits for them, and re-layouts  71.1 us (11%)
  starting transfers between devices  22.1 us (3%)
  between operations  16.6 us (2%)
    psum x1, waiting for transfers between devices, plain_sum(): return lax.psum(share, 'seq')  80.7 us
    pallas_call x1, Pallas kernels, scan_backward(): pl.pallas_call(backward_kernel, grid=(pairs, spans), in_specs=[wide, thin...  66.4 us
    all_to_all x2, blocking collectives, swap(): return lax.all_to_all(array, axis, 0, 0, tiled=True)  62.6 us
    pallas_call x1, Pallas kernels, scan_forward(): pl.pallas_call(forward_kernel, grid=(pairs, spans), in_specs=[wide, thin,...  41.5 us
    psum x1, blocking collectives, on_device(): small = lax.psum(small, ('fsdp', 'seq'))  39.7 us
    unnamed x2, blocking collectives  39 us
    all_to_all x4, waiting for transfers between devices, swap(): return lax.all_to_all(array, axis, 0, 0, tiled=True)  38.6 us
    unnamed x103, local copies, waits for them, and re-layouts  24.2 us
  transfers between devices with their start and end apart: 12, of which 6 were waited for; matrix products, arithmetic and copies ran while one was open for 21% of the time, Pallas kernels for 16%

profile of v1, /device:TPU:0, one launch (start us, length us, event | category | flops | bytes accessed | tf_op | source)
XLA Modules:
  0.0 667.2 jit_solution(7626582877113991344)
XLA Ops:
  9.0 1.2 dynamic-slice
  10.9 4.1 concatenate.25
  15.3 13.5 %all-reduce = bf16[11336]{0:T(1024)(128)(2,1)S(1)} all-reduce(bf16[11336]{0:T(1024)(128)(2,1)S(1)} %dynamic-update-slice), channel_id=2, replica_groups=mesh['seq'=8,'fsdp'=4] {'fsdp'}, use_global_device_ids=true, to_apply=%add | all-reduce | flops 11336 | bytes 45344
  29.1 0.9 reshape_reshape.6
  30.4 1.8 slice_reduce_fusion.3
  33.2 20.2 %all-gather.6.cloned.1.call-done = bf16[768,3352]{1,0:T(8,128)(2,1)} async-done(((bf16[192,3352]{1,0:T(8,128)(2,1)}), bf16[768,3352]{1,0:T(8,128)(2,1)}) %all-gather.6.cloned.1.call-update) | async-done | bytes 5148688 | tf_op jit(solution)/shard_map/all_gather | solution.py:295
  53.5 8.8 %convolution_convert_fusion = bf16[1024,3352]{1,0:T(8,128)(2,1)S(1)} fusion(bf16[768,3352]{1,0:T(8,128)(2,1)} %all-gather.6.cloned.1.call-done, bf16[1,1024,768]{2,1,0:T(8,128)(2,1)S(1)} %copy-done.12, f32[768]{0:T(1024)S(1)} %mul.306, f32[1024]{0:T(1024)S(1)} %get-tuple-element.116), kind=kOutput, calls=%fused_computation.6 | convolution fusion | flops 5278818304 | bytes 13593600 | tf_op jit(solution)/shard_map/dot_general | solution.py:313
  62.3 2.8 copy-done.10
  65.7 2.3 reduce-window.14
  68.7 3.9 collective-permute-start
  72.9 1.6 fusion.53
  74.5 4.4 fusion.56
  78.9 2.1 slice.214
  81.0 18.0 %concatenate.26 = bf16[1040,1792]{1,0:T(8,128)(2,1)} concatenate(bf16[13,1792]{1,0:T(8,128)(2,1)S(1)} %broadcast_in_dim.64, bf16[3,1792]{1,0:T(4,128)(2,1)S(1)} %collective-permute-done, bf16[1024,1792]{1,0:T(8,128)(2,1)} %slice.214), dimensions={0} | concatenate | bytes 7454720 | tf_op jit(solution)/shard_map/concatenate | solution.py:320
  99.0 2.6 convert_element_type.60
  101.6 7.6 %fusion.10 = (f32[1024,1792]{1,0:T(8,128)}, f32[1024,1792]{1,0:T(8,128)}) fusion(f32[1040,1792]{1,0:T(8,128)S(1)} %convert_element_type.60, f32[1792]{0:T(1024)S(1)} %get-tuple-element.88, f32[1792]{0:T(1024)S(1)} %get-tuple-element.89, f32[1792]{0:T(1024)S(1)} %get-tuple-element.90, f32[1792]{0:T(1024)S(1)} %get-tuple-element.87, f32[1792]{0:T(1024)S(1)} %add.146), kind=kLoop, calls=%fused_computation.23 | loop fusion | flops 22020096 | bytes 44076032 | tf_op jit(solution)/shard_map/jit(silu)/mul | solution.py:325
  109.3 9.4 %fusion.20 = f32[128,1536]{1,0:T(8,128)} fusion(f32[1024,1536]{1,0:T(8,128)} %fusion.56, f32[1024,1792]{1,0:T(8,128)} %get-tuple-element.100), kind=kOutput, calls=%fused_computation.48 | convolution fusion | flops 2417491968 | bytes 13893632 | tf_op jit(solution)/shard_map/dot_general | solution.py:349
  118.6 4.6 all-to-all-start
  125.5 25.6 %all-reduce.1 = f32[192]{0:T(256)S(1)} all-reduce(f32[192]{0:T(256)S(1)} %dynamic-update-slice.1), channel_id=3, replica_groups=mesh['seq'=8,'fsdp'=4] {'seq'}, use_global_device_ids=true, to_apply=%add.1 | all-reduce | flops 192 | bytes 1536
  151.6 1.3 multiply_reduce_fusion.9
  152.9 4.5 all-to-all-start.1
  158.6 5.8 slice.222.v_ref
  164.4 1.3 fusion.108
  165.7 10.0 %all-to-all-done.1 = f32[8,16,1536]{2,1,0:T(8,128)S(1)} async-done(((f32[8,16,1536]{2,1,0:T(8,128)}), f32[8,16,1536]{2,1,0:T(8,128)S(1)}, u32[]{:S(2)}, u32[]{:S(2)}) %all-to-all-start.1) | async-done | bytes 786464 | tf_op jit(solution)/shard_map/all_to_all | solution.py:240
  175.7 2.8 copy-done
  178.5 41.5 %scan_forward.1 = (f32[1024,1536]{1,0:T(8,128)S(1)}, f32[4,128,1536]{2,1,0:T(8,128)S(1)}) custom-call(f32[1024,1536]{1,0:T(8,128)S(1)} %copy-done, f32[1024,128]{1,0:T(8,128)S(1)} %get-tuple-element.105.w_ref, f32[1024,128]{1,0:T(8,128)S(1)} %get-tuple-element.104.r_ref, f32[12,4,8,256]{3,2,1,0:T(8,128)S(1)} %maximum_maximum_fusion.rows_ref, ...), custom_call_target="tpu_custom_call" | custom-call | tf_op jit(solution)/shard_map/scan_forward/pallas_call | solution.py:177
  219.9 7.4 %multiply_reduce_fusion.8 = (f32[1024]{0:T(1024)S(1)}, f32[1024,1536]{1,0:T(8,128)}) fusion(f32[1024,1536]{1,0:T(8,128)S(1)} %get-tuple-element.17, bf16[1024,3352]{1,0:T(8,128)(2,1)} %copy-done.10), kind=kLoop, calls=%fused_computation.46 | loop fusion | flops 12581888 | bytes 15732736 | tf_op jit(solution)/shard_map/reduce_sum | solution.py:354
  227.5 7.9 %multiply_reduce_fusion.4 = (f32[1536]{0:T(1024)}, f32[1024]{0:T(1024)S(1)}, f32[1024,1536]{1,0:T(8,128)S(1)}) fusion(f32[1024,1536]{1,0:T(8,128)} %get-tuple-element.99, f32[1024]{0:T(1024)S(1)} %get-tuple-element.118, f32[1536]{0:T(1024)S(1)} %mul.332, bf16[1536,768]{1,0:T(8,128)(2,1)} %all-gather.8.cloned.1.call-done, bf16[1,1024,768]{2,1,0:T(8,128)(2,1)} %param.21), kind=kOutput, calls=%fused_computation.38 | convolution fusion | flops 2425353728 | bytes 16535552 | tf_op jit(solution)/shard_map/td,id->ti/dot_general | solution.py:359
  235.4 10.0 %multiply_reduce_fusion.5 = (f32[1536]{0:T(1024)}, f32[1024,1536]{1,0:T(8,128)}, bf16[1024,1536]{1,0:T(8,128)(2,1)S(1)}) fusion(f32[1024,1792]{1,0:T(8,128)} %get-tuple-element.100, bf16[1024,3352]{1,0:T(8,128)(2,1)} %copy-done.10, f32[1024]{0:T(1024)S(1)} %broadcast_multiply_fusion.1, f32[1024,1536]{1,0:T(8,128)S(1)} %copy-done.9, ...), kind=kLoop, calls=%fused_computation.39 | loop fusion | flops 31455744 | bytes 37773312 | tf_op jit(solution)/shard_map/reduce_sum | solution.py:367
  245.4 1.6 copy-done.15
  247.0 4.6 fusion.101
  251.7 2.7 fusion.54
  254.4 8.6 %fusion.18 = f32[128,1536]{1,0:T(8,128)} fusion(f32[1024,1536]{1,0:T(8,128)S(1)} %fusion.54, f32[1024,1536]{1,0:T(8,128)} %get-tuple-element.94.gm_ref, f32[1024,1792]{1,0:T(8,128)} %get-tuple-element.100), kind=kOutput, calls=%fused_computation.41 | convolution fusion | flops 2417491968 | bytes 13893632 | tf_op jit(solution)/shard_map/dot_general | solution.py:368
  263.0 3.5 all-to-all-start.2
  266.9 17.9 %all-to-all-done.2 = f32[8,16,1536]{2,1,0:T(8,128)S(1)} async-done(((f32[8,16,1536]{2,1,0:T(8,128)}), f32[8,16,1536]{2,1,0:T(8,128)S(1)}, u32[]{:S(2)}, u32[]{:S(2)}) %all-to-all-start.2) | async-done | bytes 786464 | tf_op jit(solution)/shard_map/all_to_all | solution.py:240
  284.8 1.3 multiply_reduce_fusion.6
  286.2 3.5 all-to-all-start.3
  289.8 8.3 %fusion.43 = f32[1536,768]{1,0:T(8,128)} fusion(bf16[1,1024,768]{2,1,0:T(8,128)(2,1)} %param.21, f32[1024,1536]{1,0:T(8,128)} %get-tuple-element.99, f32[1536]{0:T(1024)S(1)} %mul.332, f32[1024]{0:T(1024)S(1)} %get-tuple-element.118), kind=kOutput, calls=%fused_computation.72 | convolution fusion | flops 2420637696 | bytes 12593152 | tf_op jit(solution)/shard_map/ti,td->id/dot_general | solution.py:358
  298.2 10.7 %all-to-all-done.3 = f32[8,16,1536]{2,1,0:T(8,128)S(1)} async-done(((f32[8,16,1536]{2,1,0:T(8,128)}), f32[8,16,1536]{2,1,0:T(8,128)S(1)}, u32[]{:S(2)}, u32[]{:S(2)}) %all-to-all-start.3) | async-done | bytes 786464 | tf_op jit(solution)/shard_map/all_to_all | solution.py:240
  308.9 3.4 copy-done.1
  312.3 1.9 copy-done.6
  314.2 66.4 %scan_backward.1 = (f32[1024,1536]{1,0:T(8,128)S(1)}, f32[1024,128]{1,0:T(8,128)S(1)}, f32[1024,128]{1,0:T(8,128)S(1)}, f32[12,4,8,256]{3,2,1,0:T(8,128)S(1)}) custom-call(f32[1024,1536]{1,0:T(8,128)S(1)} %copy-done.1, f32[1024,128]{1,0:T(8,128)S(1)} %get-tuple-element.105.w_ref, f32[1024,128]{1,0:T(8,128)S(1)} %get-tuple-element.104.r_ref, ...), custom_call_target="tpu_custom_call" | custom-call | tf_op jit(solution)/shard_map/scan_backward/pallas_call | solution.py:206
  380.6 2.6 copy-done.4
  384.6 4.6 reduce-window.16
  390.2 1.0 slice_add_fusion.1
  392.5 17.5 %multiply_reduce_fusion.3 = (f32[1792]{0:T(1024)}, f32[1792]{0:T(1024)}, f32[1792]{0:T(1024)}, f32[1792]{0:T(1024)}, f32[1792]{0:T(1024)}, /*index=5*/f32[1024,1792]{1,0:T(8,128)S(1)}) fusion(f32[1040,1792]{1,0:T(8,128)} %copy-done.8, f32[1024,1792]{1,0:T(8,128)} %get-tuple-element.101, f32[1024,128]{1,0:T(8,128)S(1)} %get-tuple-element.21, ...), kind=kLoop, calls=%fused_computation.21 | loop fusion | flops 34856192 | bytes 51416064 | tf_op jit(solution)/shard_map/reduce_sum | solution.py:392
  410.0 1.4 collective-permute-start.1
  411.5 1.5 fusion.106
  413.0 2.9 collective-permute-done.1
  415.9 7.1 %fusion.6 = bf16[1024,1792]{1,0:T(8,128)(2,1)S(1)} fusion(f32[3,1792]{1,0:T(4,128)S(1)} %collective-permute-done.1, f32[1024,1792]{1,0:T(8,128)S(1)} %get-tuple-element.97, f32[1792]{0:T(1024)S(1)} %copy-done.23, f32[1792]{0:T(1024)S(1)} %copy-done.25, f32[1792]{0:T(1024)S(1)} %copy-done.27, f32[1792]{0:T(1024)S(1)} %copy-done.21), kind=kLoop, calls=%fused_computation.12 | loop fusion | flops 20185088 | bytes 11060224 | tf_op jit(solution)/shard_map/convert.2
  423.1 1.8 copy-done.16
  424.9 4.9 convolution_convert_fusion.1
  429.9 4.6 copy.166
  434.5 40.1 %all_to_all.52 = bf16[4,192,1816]{2,1,0:T(8,128)(2,1)} all-to-all(bf16[4,192,1816]{2,1,0:T(8,128)(2,1)} %bitcast.116), channel_id=1, replica_groups=mesh['seq'=8,'fsdp'=4] {'fsdp'}, dimensions={0} | all-to-all | bytes 5578752 | tf_op jit(solution)/shard_map/all_to_all | solution.py:240
  474.5 2.6 reduce_sum.215
  477.2 22.5 %all_to_all.53 = bf16[8,24,1816]{2,1,0:T(8,128)(2,1)S(1)} all-to-all(bf16[8,24,1816]{2,1,0:T(8,128)(2,1)S(1)} %bitcast.117), channel_id=1, replica_groups=mesh['seq'=8,'fsdp'=4] {'seq'}, dimensions={0} | all-to-all | bytes 1394688 | tf_op jit(solution)/shard_map/all_to_all | solution.py:240
  500.8 7.3 %fusion.47 = bf16[1,1024,768]{2,1,0:T(8,128)(2,1)} fusion(bf16[1536,768]{1,0:T(8,128)(2,1)} %all-gather.8.cloned.1.call-done, bf16[1,1024,768]{2,1,0:T(8,128)(2,1)S(1)} %copy-done.14, f32[1024,1536]{1,0:T(8,128)} %get-tuple-element.99, f32[1536]{0:T(1024)S(1)} %copy-done.30, f32[1024]{0:T(1024)S(1)} %copy-done.39), kind=kOutput, calls=%fused_computation.77 | convolution fusion | flops 2422996992 | bytes 11806720 | tf_op jit(solution)/shard_map/dot_general | solution.py:356
  508.2 7.0 %fusion.36 = f32[1024,768]{1,0:T(8,128)} fusion(bf16[1024,1536]{1,0:T(8,128)(2,1)} %copy-done.15, bf16[768,3352]{1,0:T(8,128)(2,1)} %all-gather.6.cloned.1.call-done), kind=kOutput, calls=%fused_computation.67 | convolution fusion | flops 2415919104 | bytes 8650752 | tf_op jit(solution)/shard_map/tk,dk->td/dot_general | solution.py:398
  517.5 9.5 %fusion.32 = (f32[768]{0:T(1024)S(1)}, f32[1024]{0:T(1024)S(1)}, f32[1024,768]{1,0:T(8,128)}) fusion(bf16[1,1024,768]{2,1,0:T(8,128)(2,1)S(1)} %copy-done.14, f32[1024]{0:T(1024)S(1)} %get-tuple-element.116, f32[768]{0:T(1024)S(1)} %mul.306, f32[1024,768]{1,0:T(8,128)} %fusion.36, bf16[768,3352]{1,0:T(8,128)(2,1)} %all-gather.6.cloned.1.call-done, ...), kind=kOutput, calls=%fused_computation.62 | convolution fusion | flops 2870049024 | bytes 14546944 | tf_op jit(solution)/shard_map/tk,dk->td/dot_general | solution.py:400
  527.1 39.7 %psum.23 = f32[4,2834]{1,0:T(4,128)S(1)} all-reduce(f32[4,2834]{1,0:T(4,128)S(1)} %concatenate.32), channel_id=1, replica_groups=mesh['seq'=8,'fsdp'=4] {'fsdp','seq'}, use_global_device_ids=true, to_apply=%region_32.33 | all-reduce | flops 11336 | bytes 90688 | tf_op jit(solution)/shard_map/psum | solution.py:413
  570.4 3.4 fusion.42
  573.8 80.7 %all-reduce.5.cloned.1.call-done = (f32[192,1536]{1,0:T(8,128)}, f32[384,768]{1,0:T(8,128)}) async-done(((f32[192,1536]{1,0:T(8,128)}, f32[384,768]{1,0:T(8,128)}), (f32[192,1536]{1,0:T(8,128)}, f32[384,768]{1,0:T(8,128)})) %all-reduce.5.cloned.1.call-update) | async-done | bytes 2359312 | tf_op jit(solution)/shard_map/psum | solution.py:275
  654.4 3.4 pad_maximum_fusion.2
  657.8 2.4 copy.192
  (207 shorter events, 19.8 us)
Async XLA Ops:
  7.2 25.0 %copy-start.12 = (bf16[1,1024,768]{2,1,0:T(8,128)(2,1)S(1)}, bf16[1,1024,768]{2,1,0:T(8,128)(2,1)}, u32[]{:S(2)}) copy-start(bf16[1,1024,768]{2,1,0:T(8,128)(2,1)} %param.11) | copy-start | bytes 4718596
  7.2 46.3 %all-gather.6.cloned.1.call-start = ((), (), s32[]{:S(2)}) async-start(), calls=%async_computation.8 | async-start | bytes 6635520 | tf_op jit(solution)/shard_map/all_gather | solution.py:295
  29.0 33.3 %copy-start.28 = (f32[4,2834]{1,0:T(4,128)}, f32[4,2834]{1,0:T(4,128)S(1)}, u32[]{:S(2)}) copy-start(f32[4,2834]{1,0:T(4,128)S(1)} %convert_element_type.57) | copy-start | bytes 136036
  30.3 32.0 %copy-start.43 = (f32[24]{0:T(128)}, f32[24]{0:T(128)S(1)}, u32[]{:S(2)}) copy-start(f32[24]{0:T(128)S(1)} %neg.31) | copy-start | bytes 292
  30.4 42.5 %copy-start.41 = (f32[24]{0:T(128)}, f32[24]{0:T(128)S(1)}, u32[]{:S(2)}) copy-start(f32[24]{0:T(128)S(1)} %add.154) | copy-start | bytes 292
  32.2 69.4 %copy-start.20 = (f32[1792]{0:T(1024)}, f32[1792]{0:T(1024)S(1)}, u32[]{:S(2)}) copy-start(f32[1792]{0:T(1024)S(1)} %get-tuple-element.87) | copy-start | bytes 21508
  32.2 69.4 %copy-start.22 = (f32[1792]{0:T(1024)}, f32[1792]{0:T(1024)S(1)}, u32[]{:S(2)}) copy-start(f32[1792]{0:T(1024)S(1)} %get-tuple-element.88) | copy-start | bytes 21508
  32.2 69.4 %copy-start.24 = (f32[1792]{0:T(1024)}, f32[1792]{0:T(1024)S(1)}, u32[]{:S(2)}) copy-start(f32[1792]{0:T(1024)S(1)} %get-tuple-element.89) | copy-start | bytes 21508
  32.2 69.4 %copy-start.26 = (f32[1792]{0:T(1024)}, f32[1792]{0:T(1024)S(1)}, u32[]{:S(2)}) copy-start(f32[1792]{0:T(1024)S(1)} %get-tuple-element.90) | copy-start | bytes 21508
  62.3 2.9 copy-start.10
  68.7 12.3 %collective-permute-start = (bf16[3,1792]{1,0:T(4,128)(2,1)S(1)}, bf16[3,1792]{1,0:T(4,128)(2,1)S(1)}, u32[]{:S(2)}, u32[]{:S(2)}) collective-permute-start(bf16[3,1792]{1,0:T(4,128)(2,1)S(1)} %slice.213), channel_id=1, source_target_pairs={{0,4},{4,8},{8,12},{12,16},{16,20},{20,24},{24,28},{1,5},{5,9},{9,... | collective-permute-start | bytes 32264 | tf_op jit(solution)/shard_map/ppermute | solution.py:236
  72.9 6.0 copy-start.11
  101.6 7.7 %copy-start.8 = (f32[1040,1792]{1,0:T(8,128)}, f32[1040,1792]{1,0:T(8,128)S(1)}, u32[]{:S(2)}) copy-start(f32[1040,1792]{1,0:T(8,128)S(1)} %convert_element_type.60) | copy-start | bytes 22364164
  109.3 14.7 %copy-start.45 = (u32[32]{0:T(128)S(1)}, u32[32]{0:T(128)}, u32[]{:S(2)}) copy-start(u32[32]{0:T(128)} %constant.78) | copy-start | bytes 388
  118.6 32.9 %all-to-all-start = ((f32[8,16,1536]{2,1,0:T(8,128)}), f32[8,16,1536]{2,1,0:T(8,128)S(1)}, u32[]{:S(2)}, u32[]{:S(2)}) async-start(f32[8,16,1536]{2,1,0:T(8,128)} %bitcast.13), calls=%async_computation | async-start | bytes 1572864 | tf_op jit(solution)/shard_map/all_to_all | solution.py:240
  123.3 104.2 %all-gather.8.cloned.1.call-start = ((), (), s32[]{:S(2)}) async-start(), calls=%async_computation.9 | async-start | bytes 2949120 | tf_op jit(solution)/shard_map/all_gather | solution.py:296
  152.9 22.8 %all-to-all-start.1 = ((f32[8,16,1536]{2,1,0:T(8,128)}), f32[8,16,1536]{2,1,0:T(8,128)S(1)}, u32[]{:S(2)}, u32[]{:S(2)}) async-start(f32[8,16,1536]{2,1,0:T(8,128)} %multiply_reduce_fusion.9), calls=%async_computation.1 | async-start | bytes 1572864 | tf_op jit(solution)/shard_map/all_to_all | solution.py:240
  157.4 350.6 %reduce-scatter.3.cloned.1.call-start = ((), (), s32[]{:S(2)}) async-start(), calls=%async_computation.10 | async-start | bytes 5898240 | tf_op jit(solution)/shard_map/reduce_scatter | solution.py:274
  157.9 131.9 %copy-start.29 = (f32[1536]{0:T(1024)}, f32[1536]{0:T(1024)S(1)}, u32[]{:S(2)}) copy-start(f32[1536]{0:T(1024)S(1)} %mul.332) | copy-start | bytes 18436
  175.7 2.8 copy-start
  219.9 7.5 %copy-start.2 = (f32[1024,1536]{1,0:T(8,128)}, f32[1024,1536]{1,0:T(8,128)S(1)}, u32[]{:S(2)}) copy-start(f32[1024,1536]{1,0:T(8,128)S(1)} %get-tuple-element.17) | copy-start | bytes 18874372
  219.9 7.5 %copy-start.5 = (f32[4,128,1536]{2,1,0:T(8,128)}, f32[4,128,1536]{2,1,0:T(8,128)S(1)}, u32[]{:S(2)}) copy-start(f32[4,128,1536]{2,1,0:T(8,128)S(1)} %get-tuple-element.18.ent_ref) | copy-start | bytes 9437188
  227.4 62.4 %copy-start.38 = (f32[1024]{0:T(1024)}, f32[1024]{0:T(1024)S(1)}, u32[]{:S(2)}) copy-start(f32[1024]{0:T(1024)S(1)} %get-tuple-element.118) | copy-start | bytes 12292
  227.4 8.0 %copy-start.3 = (f32[1024,1536]{1,0:T(8,128)S(1)}, f32[1024,1536]{1,0:T(8,128)}, u32[]{:S(2)}) copy-start(f32[1024,1536]{1,0:T(8,128)} %copy-done.2) | copy-start | bytes 18874372
  227.5 7.9 %copy-start.9 = (f32[1024,1536]{1,0:T(8,128)S(1)}, f32[1024,1536]{1,0:T(8,128)}, u32[]{:S(2)}) copy-start(f32[1024,1536]{1,0:T(8,128)} %get-tuple-element.99) | copy-start | bytes 18874372
  235.4 11.6 %copy-start.13 = (bf16[1,1024,768]{2,1,0:T(8,128)(2,1)S(1)}, bf16[1,1024,768]{2,1,0:T(8,128)(2,1)}, u32[]{:S(2)}) copy-start(bf16[1,1024,768]{2,1,0:T(8,128)(2,1)} %param.11) | copy-start | bytes 4718596
  245.4 1.6 copy-start.15
  263.0 21.9 %all-to-all-start.2 = ((f32[8,16,1536]{2,1,0:T(8,128)}), f32[8,16,1536]{2,1,0:T(8,128)S(1)}, u32[]{:S(2)}, u32[]{:S(2)}) async-start(f32[8,16,1536]{2,1,0:T(8,128)} %bitcast.17), calls=%async_computation.2 | async-start | bytes 1572864 | tf_op jit(solution)/shard_map/all_to_all | solution.py:240
  286.2 22.7 %all-to-all-start.3 = ((f32[8,16,1536]{2,1,0:T(8,128)}), f32[8,16,1536]{2,1,0:T(8,128)S(1)}, u32[]{:S(2)}, u32[]{:S(2)}) async-start(f32[8,16,1536]{2,1,0:T(8,128)} %multiply_reduce_fusion.6), calls=%async_computation.3 | async-start | bytes 1572864 | tf_op jit(solution)/shard_map/all_to_all | solution.py:240
  289.8 218.3 %reduce-scatter.5.cloned.1.call-start = ((), (), s32[]{:S(2)}) async-start(), calls=%async_computation.12 | async-start | bytes 5898240 | tf_op jit(solution)/shard_map/reduce_scatter | solution.py:274
  298.2 275.6 %all-gather.10.cloned.1.call-start = ((), (), s32[]{:S(2)}) async-start(), calls=%async_computation.11 | async-start | bytes 1658880 | tf_op jit(solution)/shard_map/all_gather | solution.py:270
  308.9 3.4 copy-start.1
  312.3 1.9 copy-start.6
  380.6 2.6 copy-start.4
  383.2 0.7 copy-start.7
  392.5 19.0 %copy-start.42 = (f32[24]{0:T(128)S(1)}, f32[24]{0:T(128)}, u32[]{:S(2)}) copy-start(f32[24]{0:T(128)} %copy-done.41) | copy-start | bytes 292
  392.5 19.0 %copy-start.44 = (f32[24]{0:T(128)S(1)}, f32[24]{0:T(128)}, u32[]{:S(2)}) copy-start(f32[24]{0:T(128)} %copy-done.43) | copy-start | bytes 292
  392.5 23.4 %copy-start.21 = (f32[1792]{0:T(1024)S(1)}, f32[1792]{0:T(1024)}, u32[]{:S(2)}) copy-start(f32[1792]{0:T(1024)} %copy-done.20) | copy-start | bytes 21508
  392.5 23.4 %copy-start.23 = (f32[1792]{0:T(1024)S(1)}, f32[1792]{0:T(1024)}, u32[]{:S(2)}) copy-start(f32[1792]{0:T(1024)} %copy-done.22) | copy-start | bytes 21508
  392.5 23.4 %copy-start.25 = (f32[1792]{0:T(1024)S(1)}, f32[1792]{0:T(1024)}, u32[]{:S(2)}) copy-start(f32[1792]{0:T(1024)} %copy-done.24) | copy-start | bytes 21508
  392.5 23.4 %copy-start.27 = (f32[1792]{0:T(1024)S(1)}, f32[1792]{0:T(1024)}, u32[]{:S(2)}) copy-start(f32[1792]{0:T(1024)} %copy-done.26) | copy-start | bytes 21508
  410.0 14.9 %copy-start.14 = (bf16[1,1024,768]{2,1,0:T(8,128)(2,1)S(1)}, bf16[1,1024,768]{2,1,0:T(8,128)(2,1)}, u32[]{:S(2)}) copy-start(bf16[1,1024,768]{2,1,0:T(8,128)(2,1)} %param.11) | copy-start | bytes 4718596
  410.0 5.9 collective-permute-start.1
  413.0 16.9 %copy-start.18 = (bf16[1024,24]{1,0:T(8,128)(2,1)}, bf16[1024,24]{1,0:T(8,128)(2,1)S(1)}, u32[]{:S(2)}) copy-start(bf16[1024,24]{1,0:T(8,128)(2,1)S(1)} %get-tuple-element.96) | copy-start | bytes 147460
  423.1 1.8 copy-start.16
  434.5 66.3 %copy-start.30 = (f32[1536]{0:T(1024)S(1)}, f32[1536]{0:T(1024)}, u32[]{:S(2)}) copy-start(f32[1536]{0:T(1024)} %copy-done.29) | copy-start | bytes 18436
  434.5 66.3 %copy-start.39 = (f32[1024]{0:T(1024)S(1)}, f32[1024]{0:T(1024)}, u32[]{:S(2)}) copy-start(f32[1024]{0:T(1024)} %copy-done.38) | copy-start | bytes 12292
  500.5 153.9 %all-reduce.5.cloned.1.call-start = ((), (), s32[]{:S(2)}) async-start(), calls=%async_computation.13 | async-start | bytes 4718592 | tf_op jit(solution)/shard_map/psum | solution.py:275
  508.1 7.0 %copy-start.31 = (f32[1536]{0:T(1024)S(1)}, f32[1536]{0:T(1024)}, u32[]{:S(2)}) copy-start(f32[1536]{0:T(1024)} %get-tuple-element.93) | copy-start | bytes 18436
  508.1 7.3 %copy-start.40 = (f32[1536]{0:T(1024)S(1)}, f32[1536]{0:T(1024)}, u32[]{:S(2)}) copy-start(f32[1536]{0:T(1024)} %get-tuple-element.82) | copy-start | bytes 18436
  508.1 7.3 %copy-start.36 = (f32[1792]{0:T(1024)S(1)}, f32[1792]{0:T(1024)}, u32[]{:S(2)}) copy-start(f32[1792]{0:T(1024)} %get-tuple-element.79) | copy-start | bytes 21508
  508.1 7.3 %copy-start.35 = (f32[1792]{0:T(1024)S(1)}, f32[1792]{0:T(1024)}, u32[]{:S(2)}) copy-start(f32[1792]{0:T(1024)} %get-tuple-element.80) | copy-start | bytes 21508
  508.1 7.3 %copy-start.34 = (f32[1792]{0:T(1024)S(1)}, f32[1792]{0:T(1024)}, u32[]{:S(2)}) copy-start(f32[1792]{0:T(1024)} %get-tuple-element.81) | copy-start | bytes 21508
  508.1 7.4 %copy-start.33 = (f32[1792]{0:T(1024)S(1)}, f32[1792]{0:T(1024)}, u32[]{:S(2)}) copy-start(f32[1792]{0:T(1024)} %get-tuple-element.78) | copy-start | bytes 21508
  508.1 8.3 %copy-start.32 = (f32[1792]{0:T(1024)S(1)}, f32[1792]{0:T(1024)}, u32[]{:S(2)}) copy-start(f32[1792]{0:T(1024)} %get-tuple-element.84) | copy-start | bytes 21508
  508.1 9.3 %copy-start.19 = (bf16[1024,24]{1,0:T(8,128)(2,1)S(1)}, bf16[1024,24]{1,0:T(8,128)(2,1)}, u32[]{:S(2)}) copy-start(bf16[1024,24]{1,0:T(8,128)(2,1)} %copy-done.18) | copy-start | bytes 147460
  517.4 52.9 %copy-start.17 = (bf16[1,1024,768]{2,1,0:T(8,128)(2,1)S(1)}, bf16[1,1024,768]{2,1,0:T(8,128)(2,1)}, u32[]{:S(2)}) copy-start(bf16[1,1024,768]{2,1,0:T(8,128)(2,1)} %param.21) | copy-start | bytes 4718596
  517.4 52.9 %copy-start.37 = (f32[1024]{0:T(1024)S(1)}, f32[1024]{0:T(1024)}, u32[]{:S(2)}) copy-start(f32[1024]{0:T(1024)} %get-tuple-element.115) | copy-start | bytes 12292
Sparse Core Ops, SparseCore 0:
  9.6 43.8 all-gather.5
  125.7 24.5 all-gather.7
  251.8 45.8 reduce-scatter.2
  300.3 47.8 reduce-scatter.4
  500.6 42.1 all-gather.9
  546.3 108.1 all-reduce.4
